TPU v7x, 128 devices: a whole 4x4x4 slice. The times are simulated.
128 devices in a mesh: batch: 16 (over x, y_lo, core), aug: 8 (over y_hi, z).
Axes of the slice: x: 4, y: 4 (y_hi: 2, y_lo: 2; y = y_hi * 2 + y_lo), z: 4, core: 2. Of those that a mesh axis runs over, the one named last changes fastest.
Arguments:
- student_image: bfloat16 [8, 4608, 512], P('aug', 'batch'), may hold values from -8 to 8
- student_text: bfloat16 [4608, 512], P('batch'), may hold values from -8 to 8
- teacher_image: bfloat16 [8, 4608, 1280], P('aug', 'batch'), may hold values from -8 to 8
- teacher_text: bfloat16 [4608, 1280], P('batch'), may hold values from -8 to 8
Outputs:
- loss: float32 [], replicated
- grad_image: float32 [8, 4608, 512], P('aug', 'batch')
- grad_text: float32 [4608, 512], P('batch')
All inputs are finite; a program needn't handle non-finite values.
Results may differ from a plain program's by a relative error of at most 0.0011.
The roundings to bfloat16 on the way count: a program that leaves them out, or rounds other values in their place, can miss the bound.
Values may be sent and summed in bfloat16 or wider, within the bound.
A program may use at most 128 MiB of HBM per device.

v0:
```python
import math

import jax
import jax.numpy as jnp
from jax import lax
from jax.sharding import PartitionSpec as P


def scores(left_side, right_side, factor):
    return (
        jnp.einsum("rk,ck->rc", left_side, right_side, preferred_element_type=jnp.float32) * factor
    )


def row_lse(logits):
    top_value = jnp.max(logits, axis=1, keepdims=True)
    return top_value + jnp.log(jnp.sum(jnp.exp(logits - top_value), axis=1, keepdims=True))


def per_device(student_image, student_text, teacher_image, teacher_text):
    image_rows = student_image[0]
    teacher_views = teacher_image[0]
    row_count = image_rows.shape[0]
    views = lax.axis_size("aug")
    student_scale = 3.0 / math.sqrt(image_rows.shape[1])
    teacher_scale = 3.0 / math.sqrt(teacher_views.shape[1])
    all_texts = lax.all_gather(student_text, "batch", axis=0, tiled=True)
    pairs = all_texts.shape[0]
    teacher_logits = scores(
        teacher_views, lax.all_gather(teacher_text, "batch", axis=0, tiled=True), teacher_scale
    )
    student_logits = scores(image_rows, all_texts, student_scale)
    teacher_row_lse = row_lse(teacher_logits)
    student_row_lse = row_lse(student_logits)
    teacher_top = jnp.max(teacher_logits, axis=0)
    student_top = jnp.max(student_logits, axis=0)
    teacher_high, student_high = (
        lax.pmax(teacher_top.astype(jnp.bfloat16), "batch").astype(teacher_top.dtype),
        lax.pmax(student_top.astype(jnp.bfloat16), "batch").astype(student_top.dtype),
    )
    teacher_local = jnp.sum(jnp.exp(teacher_logits - teacher_high[None, :]), axis=0)
    student_local = jnp.sum(jnp.exp(student_logits - student_high[None, :]), axis=0)
    teacher_total, student_total = lax.psum((teacher_local, student_local), "batch")
    teacher_col_lse = teacher_high + jnp.log(teacher_total)
    student_col_lse = student_high + jnp.log(student_total)
    own_targets = jnp.exp(teacher_logits - teacher_row_lse) + jnp.exp(
        teacher_logits - teacher_col_lse[None, :]
    )
    weights = (
        jnp.exp(student_logits - student_row_lse)
        + jnp.exp(student_logits - student_col_lse[None, :])
    ).astype(jnp.bfloat16)
    target_weights = (lax.psum(own_targets, "aug") / views).astype(jnp.bfloat16)
    target_text = jnp.dot(target_weights, all_texts, preferred_element_type=jnp.float32)
    grad_image = (
        (jnp.dot(weights, all_texts, preferred_element_type=jnp.float32) - target_text)
        * student_scale
    )[None]
    block = weights
    own_term = jnp.einsum("rc,rk->ck", block, image_rows, preferred_element_type=jnp.float32)
    block = target_weights
    partial_sum = lax.psum_scatter(
        (own_term - jnp.einsum("rc,rk->ck", block, image_rows, preferred_element_type=jnp.float32))
        * student_scale,
        "batch",
        scatter_dimension=0,
        tiled=True,
    )
    grad_text = lax.psum(partial_sum, "aug")
    own_columns = lax.dynamic_slice_in_dim(
        student_col_lse, lax.axis_index("batch") * row_count, row_count, 0
    )
    target_loss = jnp.sum(image_rows.astype(jnp.float32) * target_text) * student_scale
    local_loss = -target_loss + jnp.sum(student_row_lse) + jnp.sum(own_columns)
    loss = lax.psum(local_loss, ("batch", "aug")) / (2.0 * views * pairs)
    return (loss, grad_image, grad_text)


def solution(mesh):
    return jax.shard_map(
        per_device,
        mesh=mesh,
        in_specs=(
            P("aug", "batch", None),
            P("batch", None),
            P("aug", "batch", None),
            P("batch", None),
        ),
        out_specs=(P(), P("aug", "batch", None), P("batch", None)),
        check_vma=False,
    )
```

profile of v0, /device:TPU:97, one launch (start us, length us, event | category | flops | bytes accessed | tf_op | source)
XLA Modules:
  0.0 585.1 jit_solution(12176179530309008169)
XLA Ops:
  7.2 0.0 copy-start
  7.2 0.0 all-gather.5.cloned.1.call-start
  7.2 0.7 all-gather.5.cloned.1.call-update
  7.9 0.0 all-gather.3.cloned.1.call-start
  8.0 0.7 all-gather.3.cloned.1.call-update
  8.7 0.0 all-reduce.5.cloned.1.call-start
  8.7 41.1 %all-gather.5.cloned.1.call-done = bf16[4608,512]{1,0:T(8,128)(2,1)} async-done(((bf16[288,512]{1,0:T(8,128)(2,1)}), bf16[4608,512]{1,0:T(8,128)(2,1)}) %all-gather.5.cloned.1.call-update) | async-done | bytes 4718608 | tf_op jit(solution)/shard_map/all_gather | solution.py:27
  49.8 6.3 %fusion.10 = (bf16[4608]{0:T(1024)(128)(2,1)S(1)}, f32[288]{0:T(512)S(1)}, f32[288,4608]{1,0:T(8,128)}) fusion(bf16[4608,512]{1,0:T(8,128)(2,1)} %all-gather.5.cloned.1.call-done, bf16[1,288,512]{2,1,0:T(8,128)(2,1)} %param.4), kind=kOutput, calls=%fused_computation.27 | convolution fusion | flops 1362930944 | bytes 10332288 | tf_op jit(solution)/shard_map/rk,ck->rc/dot_general | solution.py:11
  56.2 63.7 %all-gather.3.cloned.1.call-done = bf16[4608,1280]{1,0:T(8,128)(2,1)} async-done(((bf16[288,1280]{1,0:T(8,128)(2,1)}), bf16[4608,1280]{1,0:T(8,128)(2,1)}) %all-gather.3.cloned.1.call-update) | async-done | bytes 11796496 | tf_op jit(solution)/shard_map/all_gather | solution.py:30
  119.9 0.0 copy-done
  119.9 10.3 %fusion.11 = (f32[288]{0:T(512)S(1)}, bf16[4608]{0:T(1024)(128)(2,1)S(1)}, f32[288,4608]{1,0:T(8,128)}) fusion(bf16[4608,1280]{1,0:T(8,128)(2,1)} %all-gather.3.cloned.1.call-done, bf16[1,288,1280]{2,1,0:T(8,128)(2,1)S(1)} %copy-done), kind=kOutput, calls=%fused_computation.28 | convolution fusion | flops 3401362688 | bytes 17852544 | tf_op jit(solution)/shard_map/rk,ck->rc/dot_general | solution.py:11
  130.2 51.3 %all-reduce.1 = (bf16[4608]{0:T(1024)(128)(2,1)S(1)}, bf16[4608]{0:T(1024)(128)(2,1)S(1)}) all-reduce(bf16[4608]{0:T(1024)(128)(2,1)S(1)} %get-tuple-element.10, bf16[4608]{0:T(1024)(128)(2,1)S(1)} %get-tuple-element.5), channel_id=1, replica_groups=mesh['batch'=16,'aug'=8] {'batch'}, use_global_device_ids=true, to_apply=%region_3.0 | all-reduce | flops 9216 | bytes 36864 | tf_op jit(solution)/shard_map/pmax | solution.py:38
  181.5 5.8 exponential_reduce_fusion
  187.3 53.0 %all-reduce = (f32[4608]{0:T(1024)S(1)}, f32[4608]{0:T(1024)S(1)}) all-reduce(f32[4608]{0:T(1024)S(1)} %get-tuple-element.21, f32[4608]{0:T(1024)S(1)} %get-tuple-element.3), channel_id=1, replica_groups=mesh['batch'=16,'aug'=8] {'batch'}, use_global_device_ids=true, to_apply=%region_5.0 | all-reduce | flops 9216 | bytes 73728 | tf_op jit(solution)/shard_map/psum | solution.py:43
  240.4 6.3 %exponential_add_fusion = f32[288,4608]{1,0:T(8,128)} fusion(f32[288,4608]{1,0:T(8,128)} %get-tuple-element.17, f32[4608]{0:T(1024)S(1)} %log_add_fusion.1, f32[288]{0:T(512)S(1)} %log_add_fusion.3), kind=kLoop, calls=%fused_computation.7 | loop fusion | flops 3981312 | bytes 10636416 | tf_op jit(solution)/shard_map/add | solution.py:46
  246.6 0.0 copy-start.1
  246.6 0.0 all-reduce.5.cloned.1.call-update
  246.7 0.2 reduce-scatter.2.cloned.1.call-start
  246.9 0.6 fusion.12
  247.5 0.1 copy-done.1
  247.6 9.4 %fusion.5 = f32[4608,512]{1,0:T(8,128)} fusion(bf16[1,288,512]{2,1,0:T(8,128)(2,1)S(1)} %copy-done.1, f32[288,4608]{1,0:T(8,128)} %get-tuple-element.18, f32[4608]{0:T(1024)S(1)} %log_add_fusion, f32[288]{0:T(512)S(1)} %get-tuple-element.16), kind=kOutput, calls=%fused_computation.17 | convolution fusion | flops 1364262912 | bytes 15060096 | tf_op jit(solution)/shard_map/rc,rk->ck/dot_general | solution.py:60
  257.0 117.9 %all-reduce.5.cloned.1.call-done = f32[288,4608]{1,0:T(8,128)} async-done(((f32[288,4608]{1,0:T(8,128)}), f32[288,4608]{1,0:T(8,128)}) %all-reduce.5.cloned.1.call-update) | async-done | bytes 5308432 | tf_op jit(solution)/shard_map/psum | solution.py:53
  374.9 9.1 %subtract_multiply_fusion = f32[4608,512]{1,0:T(8,128)} fusion(f32[4608,512]{1,0:T(8,128)} %fusion.5, f32[288,4608]{1,0:T(8,128)} %all-reduce.5.cloned.1.call-done, bf16[1,288,512]{2,1,0:T(8,128)(2,1)S(1)} %copy-done.1), kind=kOutput, calls=%fused_computation | convolution fusion | flops 1366327296 | bytes 24477696 | tf_op jit(solution)/shard_map/rc,rk->ck/dot_general | solution.py:63
  384.0 0.0 reduce-scatter.2.cloned.1.call-update
  384.0 0.0 all-reduce.7.cloned.1.call-start
  384.1 0.7 dynamic-slice_reduce_fusion
  384.8 6.1 %multiply_reduce_fusion = (f32[]{:T(128)}, f32[288,512]{1,0:T(8,128)S(1)}) fusion(bf16[1,288,512]{2,1,0:T(8,128)(2,1)S(1)} %copy-done.1, bf16[4608,512]{1,0:T(8,128)(2,1)} %all-gather.5.cloned.1.call-done, f32[288,4608]{1,0:T(8,128)} %all-reduce.5.cloned.1.call-done), kind=kOutput, calls=%fused_computation.15 | convolution fusion | flops 1362051072 | bytes 10911748 | tf_op jit(solution)/shard_map/dot_general | solution.py:54
  392.8 69.3 %psum.38 = f32[]{:T(128)} all-reduce(f32[]{:T(128)S(6)} %add.57), channel_id=1, replica_groups=mesh['batch'=16,'aug'=8] {'batch','aug'}, use_global_device_ids=true, to_apply=%region_16.0 | all-reduce | flops 1 | bytes 8 | tf_op jit(solution)/shard_map/psum | solution.py:75
  462.8 31.3 %reduce-scatter.2.cloned.1.call-done = f32[288,512]{1,0:T(8,128)} async-done(((f32[4608,512]{1,0:T(8,128)}), f32[288,512]{1,0:T(8,128)}) %reduce-scatter.2.cloned.1.call-update) | async-done | bytes 589840 | tf_op jit(solution)/shard_map/reduce_scatter | solution.py:62
  494.1 0.0 all-reduce.7.cloned.1.call-update
  494.1 6.4 %fusion.1 = f32[1,288,512]{2,1,0:T(8,128)} fusion(f32[288,512]{1,0:T(8,128)S(1)} %get-tuple-element.20, bf16[4608,512]{1,0:T(8,128)(2,1)} %all-gather.5.cloned.1.call-done, f32[288,4608]{1,0:T(8,128)} %get-tuple-element.18, f32[4608]{0:T(1024)S(1)} %log_add_fusion, f32[288]{0:T(512)S(1)} %get-tuple-element.16), kind=kOutput, calls=%fused_computation.12 | convolution fusion | flops 1364557824 | bytes 11226240 | tf_op jit(solution)/shard_map/dot_general | solution.py:56
  500.5 75.0 %all-reduce.7.cloned.1.call-done = f32[288,512]{1,0:T(8,128)} async-done(((f32[288,512]{1,0:T(8,128)}), f32[288,512]{1,0:T(8,128)}) %all-reduce.7.cloned.1.call-update) | async-done | bytes 589840 | tf_op jit(solution)/shard_map/psum | solution.py:69
  575.5 1.9 copy.9
  (5 shorter events, 0.0 us)
Async XLA Ops:
  7.2 112.7 %copy-start = (bf16[1,288,1280]{2,1,0:T(8,128)(2,1)S(1)}, bf16[1,288,1280]{2,1,0:T(8,128)(2,1)}, u32[]{:S(2)}) copy-start(bf16[1,288,1280]{2,1,0:T(8,128)(2,1)} %param.6) | copy-start | bytes 2211844
  7.2 42.6 %all-gather.5.cloned.1.call-start = ((), (), s32[]{:S(2)}) async-start(), calls=%async_computation.3 | async-start | bytes 5013504 | tf_op jit(solution)/shard_map/all_gather | solution.py:27
  7.9 112.0 %all-gather.3.cloned.1.call-start = ((), (), s32[]{:S(2)}) async-start(), calls=%async_computation.1 | async-start | bytes 12533760 | tf_op jit(solution)/shard_map/all_gather | solution.py:30
  8.7 366.2 %all-reduce.5.cloned.1.call-start = ((), (), s32[]{:S(2)}) async-start(), calls=%async_computation.2 | async-start | bytes 10616832 | tf_op jit(solution)/shard_map/psum | solution.py:53
  246.6 1.0 copy-start.1
  246.7 247.4 %reduce-scatter.2.cloned.1.call-start = ((), (), s32[]{:S(2)}) async-start(), calls=%async_computation.4 | async-start | bytes 10027008 | tf_op jit(solution)/shard_map/reduce_scatter | solution.py:62
  384.0 191.5 %all-reduce.7.cloned.1.call-start = ((), (), s32[]{:S(2)}) async-start(), calls=%async_computation.5 | async-start | bytes 1179648 | tf_op jit(solution)/shard_map/psum | solution.py:69
Sparse Core Ops, SparseCore 0:
  9.7 40.0 all-gather.4
  51.5 68.3 all-gather.2
  246.8 128.0 all-reduce.4
  384.1 109.8 reduce-scatter.1
  496.4 79.0 all-reduce.6
where the time goes:
time: 594 us; the launch traced here: 585 us
  waiting for transfers between devices  330 us (56%)
  blocking collectives  174 us (29%)
  matrix products  47.7 us (8%)
  between operations  17.5 us (3%)
  other arithmetic  13.4 us (2%)
    psum x1, waiting for transfers between devices, per_device(): target_weights = (lax.psum(own_targets, 'aug') / views).astype(jnp.bfloat16)  118 us
    psum x1, waiting for transfers between devices, per_device(): grad_text = lax.psum(partial_sum, 'aug')  75 us
    psum x1, blocking collectives, per_device(): loss = lax.psum(local_loss, ('batch', 'aug')) / (2.0 * views * pairs)  69.3 us
    all_gather x1, waiting for transfers between devices, per_device(): lax.all_gather(teacher_text, 'batch', axis=0, tiled=True)  63.7 us
    psum x1, blocking collectives, per_device(): lax.psum((teacher_local, student_local), 'batch')  53 us
    pmax x1, blocking collectives, per_device(): lax.pmax(teacher_top.astype(jnp.bfloat16), 'batch')  51.3 us
    all_gather x1, waiting for transfers between devices, per_device(): all_texts = lax.all_gather(student_text, 'batch', axis=0, tiled=True)  41.1 us
    reduce_scatter x1, waiting for transfers between devices, per_device(): lax.psum_scatter((own_term - jnp.einsum('rc,rk->ck', block, image_rows, p...  31.3 us
  transfers between devices with their start and end apart: 5, of which 5 were waited for; matrix products, arithmetic and copies ran while one was open for 5% of the time, Pallas kernels for 0%

commit v1 on v0

v1 whole, which is shorter than its diff:
```python
import functools
import math

import jax
import jax.numpy as jnp
from jax import lax
from jax.experimental import pallas as pl
from jax.experimental.pallas import tpu as pltpu
from jax.sharding import PartitionSpec as P

MESH = pl.DeviceIdType.MESH
F32 = jnp.float32
BF16 = jnp.bfloat16
ROWS = 288
HALF = ROWS // 2
CH = 384
NCH = 3
NT = (((1,), (1,)), ((), ()))
NN = (((1,), (0,)), ((), ()))
TN = (((0,), (0,)), ((), ()))


def dot(a, b, dims):
    return lax.dot_general(a, b, dims, preferred_element_type=F32)


def kernel(
    simg, stext, timg, ttext,
    loss_out, gi_out, gt_out,
    it, is_, tt, ts, pt, qt, ps, qs, w, tgt, tgt_in, tw,
    gsend, grecv, gtp, gt_sib, rs_buf, fb_src, fb_buf, gtc,
    rowst, rowsend, rowrecv, rowfac, rowtmp, colst, colrecv, colfac, collse,
    loss_src, loss_b, loss_src2, loss_a,
    zi_s, zi_r, t1_s, t1_r, t2_s, t2_r, t3_s, t3_r,
    row_s, row_r, col_s, col_r, tgt_s, tgt_r, g_s, g_r, gc_s, gc_r,
    rs_s, rs_r, fb_s, fb_r, lb_s, lb_r, la_s, la_r,
):
    b = lax.axis_index("batch")
    a = lax.axis_index("aug")
    x, j = b // 4, b % 4
    yl, k = j // 2, j % 2
    yh, z = a // 4, a % 4
    sib = (b + 1 - 2 * k, a)
    teacher_scale = 3.0 / math.sqrt(timg.shape[1])
    student_scale = 3.0 / math.sqrt(simg.shape[1])

    def dev(x_, j_, yh_, z_):
        return (x_ * 4 + j_, yh_ * 4 + z_)

    def znext(d):
        return (b, yh * 4 + lax.rem(z + d, 4))

    def copy(src, dst, ss, rs, to):
        return pltpu.make_async_remote_copy(
            src_ref=src, dst_ref=dst, send_sem=ss, recv_sem=rs, device_id=to, device_id_type=MESH
        )

    barrier = pltpu.get_barrier_semaphore()

    def greet_plane(d, _):
        i = lax.rem(b * 2 + yh + d, 32)
        pl.semaphore_signal(barrier, 1, device_id=(i // 2, (i % 2) * 4 + z), device_id_type=MESH)
        return 0

    lax.fori_loop(1, 32, greet_plane, 0)

    def greet_line(d, _):
        dz, i = d // 8 + 1, d % 8
        pl.semaphore_signal(
            barrier, 1, device_id=dev(x, i // 2, i % 2, lax.rem(z + dz, 4)), device_id_type=MESH
        )
        return 0

    lax.fori_loop(0, 24, greet_line, 0)
    pl.semaphore_wait(barrier, 55)

    zm1, zp1, zp2 = lax.rem(z + 3, 4), lax.rem(z + 1, 4), lax.rem(z + 2, 4)
    own = (timg, simg)
    imgs = (it, is_)
    texts = (tt, ts)
    own_text = (ttext, stext)

    def half(h):
        return pl.ds(h * HALF, HALF)

    def img_send(m, d, h):
        return copy(
            own[m].at[half(h)], imgs[m].at[z, half(h)], zi_s.at[m, d, h], zi_r.at[m, d, h],
            znext(1 if d == 0 else 3),
        )

    def img_relay(m, d):
        slot = zm1 if d == 0 else zp1
        ref = imgs[m].at[slot, half(d)]
        return copy(ref, ref, zi_s.at[m, 2, d], zi_r.at[m, 2, d], znext(1 if d == 0 else 3))

    def img_recv(m, d, h):
        slot = zm1 if d == 0 else zp1
        ref = imgs[m].at[slot, half(h)]
        copy(ref, ref, zi_s.at[m, d, h], zi_r.at[m, d, h], znext(1)).wait_recv()

    def img_recv_far(m, d):
        ref = imgs[m].at[zp2, half(d)]
        copy(ref, ref, zi_s.at[m, 2, d], zi_r.at[m, 2, d], znext(1)).wait_recv()

    def img_start(m):
        img_send(m, 0, 0).start()
        img_send(m, 1, 1).start()
        img_send(m, 0, 1).start()
        img_send(m, 1, 0).start()

    def img_pass_on(m):
        img_recv(m, 0, 0)
        img_relay(m, 0).start()
        img_recv(m, 1, 1)
        img_relay(m, 1).start()

    syl, sk = z // 2, z % 2
    is_source = j == z

    def tslab(m, blk, h):
        return texts[m].at[pl.ds(blk * ROWS + h * HALF, HALF)]

    def text_first(m):
        return (
            copy(own_text[m].at[pl.ds((1 - sk) * HALF, HALF)], tslab(m, x, 1 - sk),
                 t1_s.at[m, 0], t1_r.at[m], dev(x, syl * 2 + 1 - sk, yh, z)),
            copy(own_text[m].at[half(0)], tslab(m, x, 0),
                 t1_s.at[m, 1], t1_r.at[m], dev(x, (1 - syl) * 2, yh, z)),
            copy(own_text[m].at[half(1)], tslab(m, x, 1),
                 t1_s.at[m, 2], t1_r.at[m], dev(x, (1 - syl) * 2 + 1, yh, z)),
        )

    def text_start(m):
        @pl.when(is_source)
        def _():
            for c in text_first(m):
                c.start()
            tslab(m, x, k)[...] = own_text[m][pl.ds(k * HALF, HALF)]

    def text_x(m, d):
        return copy(tslab(m, x, k), tslab(m, x, k), t2_s.at[m, d - 1], t2_r.at[m, d - 1],
                    (lax.rem(x + d, 4) * 4 + j, a))

    def text_sib(m, d):
        blk = lax.rem(x + 4 - d, 4)
        return copy(tslab(m, blk, k), tslab(m, blk, k), t3_s.at[m, d], t3_r.at[m, d], sib)

    def text_spread(m):
        @pl.when(jnp.logical_not(is_source))
        def _():
            copy(tslab(m, x, k), tslab(m, x, k), t1_s.at[m, 0], t1_r.at[m], sib).wait_recv()

        for d in (1, 3, 2):
            text_x(m, d).start()
        text_sib(m, 0).start()

    def text_share(m):
        for d in (1, 3, 2):
            blk = lax.rem(x + 4 - d, 4)
            copy(tslab(m, blk, k), tslab(m, blk, k), t2_s.at[m, d - 1], t2_r.at[m, d - 1],
                 sib).wait_recv()
            text_sib(m, d).start()

    def text_wait(m):
        for d in range(4):
            blk = lax.rem(x + 4 - d, 4)
            copy(tslab(m, blk, 1 - k), tslab(m, blk, 1 - k), t3_s.at[m, d], t3_r.at[m, d],
                 sib).wait_recv()

    lane = lax.broadcasted_iota(jnp.int32, (ROWS, 128), 1)

    def scores(m, v, pr, qr, scale):
        def first(n, top):
            t = dot(imgs[m][v], texts[m][pl.ds(n * CH, CH), :], NT) * scale
            cm = jnp.max(t, axis=0, keepdims=True)
            q = jnp.exp(t - cm)
            pr[v, n] = t
            qr[v, n] = q
            colst[m, n, pl.ds(v, 1), :] = cm
            colst[m, n, pl.ds(v + 4, 1), :] = jnp.sum(q, axis=0, keepdims=True)
            return jnp.maximum(
                top, jnp.maximum(jnp.maximum(t[:, :128], t[:, 128:256]), t[:, 256:])
            )

        top = lax.fori_loop(0, NCH, first, jnp.full((ROWS, 128), -jnp.inf, F32))
        top = jnp.max(top, axis=1, keepdims=True)

        def second(n, total):
            p = jnp.exp(pr[v, n] - top)
            pr[v, n] = p
            return total + (p[:, :128] + p[:, 128:256] + p[:, 256:])

        total = lax.fori_loop(0, NCH, second, jnp.zeros((ROWS, 128), F32))
        total = jnp.sum(total, axis=1, keepdims=True)
        rowst[:ROWS, :] = jnp.where(
            lane == v, top, jnp.where(lane == v + 4, total, rowst[:ROWS, :])
        )

    def row_copy(m, d):
        return copy(rowsend.at[m], rowrecv.at[m, d - 1], row_s.at[m, d - 1], row_r.at[m, d - 1],
                    znext(d))

    def col_copy(m, d):
        return copy(colst.at[m], colrecv.at[m, d - 1], col_s.at[m, d - 1], col_r.at[m, d - 1],
                    (lax.rem(b + d, 16), a))

    def stats_start(m):
        def go(d, _):
            col_copy(m, d).start()
            return 0

        lax.fori_loop(1, 16, go, 0)
        rowsend[m] = jnp.transpose(rowst[...])[:8]
        for d in (1, 3, 2):
            row_copy(m, d).start()

    def stats_finish(m):
        for d in (1, 3, 2):
            row_copy(m, d).wait_recv()
        mine = rowsend[m]
        top = mine[:4]
        for d in range(3):
            top = jnp.maximum(top, rowrecv[m, d, :4])
        total = mine[4:] * jnp.exp(mine[:4] - top)
        for d in range(3):
            got = rowrecv[m, d]
            total = total + got[4:] * jnp.exp(got[:4] - top)
        row_lse = top + jnp.log(total)
        rowtmp[0:4, :] = jnp.exp(mine[:4] - row_lse)
        rowfac[...] = jnp.transpose(rowtmp[...])

        def arrived(d, _):
            col_copy(m, d).wait_recv()
            return 0

        lax.fori_loop(1, 16, arrived, 0)
        cmine = colst[m]

        def highest(d, t):
            return jnp.maximum(t, colrecv[m, d, :, :4, :])

        ctop = lax.fori_loop(0, 15, highest, cmine[:, :4, :])

        def add(d, t):
            got = colrecv[m, d]
            return t + got[:, 4:, :] * jnp.exp(got[:, :4, :] - ctop)

        ctotal = lax.fori_loop(
            0, 15, add, cmine[:, 4:, :] * jnp.exp(cmine[:, :4, :] - ctop)
        )
        col_lse = ctop + jnp.log(ctotal)
        colfac[:, 0:4, :] = jnp.exp(cmine[:, :4, :] - col_lse)
        return row_lse, col_lse

    rowst[...] = jnp.ones_like(rowst)
    rowtmp[...] = jnp.zeros_like(rowtmp)
    img_start(0)
    text_start(0)
    it[z] = timg[...]
    is_[z] = simg[...]
    text_spread(0)
    img_pass_on(0)
    text_start(1)
    img_start(1)
    text_share(0)
    text_spread(1)
    text_wait(0)

    def view_at(i):
        return lax.rem(z + i, 4)

    scores(0, z, pt, qt, teacher_scale)
    img_pass_on(1)
    img_recv(0, 0, 1)
    scores(0, zm1, pt, qt, teacher_scale)
    img_recv(0, 1, 0)
    scores(0, zp1, pt, qt, teacher_scale)
    text_share(1)
    img_recv_far(0, 0)
    img_recv_far(0, 1)
    scores(0, zp2, pt, qt, teacher_scale)
    stats_start(0)
    stats_finish(0)

    partner = (b, (1 - yh) * 4 + z)

    def tgt_copy(n):
        return copy(tgt.at[n], tgt_in.at[n], tgt_s.at[n], tgt_r.at[n], partner)

    for n in range(NCH):
        acc = None
        for v in range(4):
            term = pt[v, n] * rowfac[:ROWS, v : v + 1] + qt[v, n] * colfac[n, v : v + 1, :]
            acc = term if acc is None else acc + term
        tgt[n] = acc
        tgt_copy(n).start()

    text_wait(1)
    scores(1, z, ps, qs, student_scale)
    img_recv(1, 0, 1)
    scores(1, zm1, ps, qs, student_scale)
    img_recv(1, 1, 0)
    scores(1, zp1, ps, qs, student_scale)
    img_recv_far(1, 0)
    img_recv_far(1, 1)
    scores(1, zp2, ps, qs, student_scale)
    stats_start(1)
    row_lse, col_lse = stats_finish(1)
    rl = lax.broadcasted_iota(jnp.int32, (4, CH), 0)
    cl = lax.broadcasted_iota(jnp.int32, (4, CH), 1)
    lse_part = jnp.sum(
        jnp.where((rl == z) & (cl < ROWS), row_lse, 0.0)
        + jnp.sum(col_lse, axis=0) * (1.0 / 16.0),
        axis=0, keepdims=True,
    )
    collse[0:1, :] = lse_part

    for v in range(4):
        for n in range(NCH):
            w[v, n] = (
                ps[v, n] * rowfac[:ROWS, v : v + 1] + qs[v, n] * colfac[n, v : v + 1, :]
            ).astype(BF16)

    def image_term(i, _):
        v = view_at(i)
        acc = dot(w[v, 0], ts[0:CH, :], NN)
        for n in range(1, NCH):
            acc = acc + dot(w[v, n], ts[n * CH : (n + 1) * CH, :], NN)
        gsend[i] = acc
        return 0

    lax.fori_loop(0, 4, image_term, 0)

    def text_term(n, _):
        acc = dot(w[0, n], is_[0], TN)
        for v in range(1, 4):
            acc = acc + dot(w[v, n], is_[v], TN)
        gtp[n] = acc
        return 0

    lax.fori_loop(0, NCH, text_term, 0)
    total_img = (
        is_[0].astype(F32) + is_[1].astype(F32) + is_[2].astype(F32) + is_[3].astype(F32)
    )
    hi = total_img.astype(BF16)
    lo = (total_img - hi.astype(F32)).astype(BF16)

    for n in range(NCH):
        tgt_copy(n).wait_recv()
        tw[n] = ((tgt[n] + tgt_in[n]) * 0.125).astype(BF16)
    target_text = dot(tw[0], ts[0:CH, :], NN)
    for n in range(1, NCH):
        target_text = target_text + dot(tw[n], ts[n * CH : (n + 1) * CH, :], NN)

    def g_copy(d):
        return copy(gsend.at[d], grecv.at[d - 1], g_s.at[d - 1], g_r.at[d - 1], znext(d))

    for d in (2, 1, 3):
        gsend[d] = gsend[d] - target_text
        g_copy(d).start()
    gsend[0] = gsend[0] - target_text

    for n in range(NCH):
        res = gtp[n] - dot(tw[n], hi, TN) - dot(tw[n], lo, TN)
        for s in range(8):
            row = n * CH + s * 48
            blk, inner = row // ROWS, row % ROWS
            kk, off = inner // HALF, inner % HALF
            for g in range(4):
                gtc[kk, blk, g, off : off + 48, :] = res[
                    s * 48 : (s + 1) * 48, g * 128 : (g + 1) * 128
                ]
    gc = copy(gtc.at[1 - k], gt_sib, gc_s.at[0], gc_r.at[0], sib)
    gc.start()

    target_loss = jnp.sum(
        jnp.sum(total_img * target_text, axis=0, keepdims=True), axis=1, keepdims=True
    )
    part = jnp.sum(collse[0:1, :], axis=1, keepdims=True) - target_loss * student_scale
    loss_src[...] = jnp.broadcast_to(part, (8, 128))

    def lb_copy(d):
        return copy(loss_src, loss_b.at[d - 1], lb_s.at[d - 1], lb_r.at[d - 1],
                    (lax.rem(b + d, 16), a))

    def lb_go(d, _):
        lb_copy(d).start()
        return 0

    lax.fori_loop(1, 16, lb_go, 0)

    gc.wait_recv()
    for blk in range(4):
        for g in range(4):
            gtc[k, blk, g] = gtc[k, blk, g] + gt_sib[blk, g]
    chip = x * 4 + yl * 2 + yh

    def rs_copy(d):
        i = lax.rem(chip + d, 16)
        xi, yli, yhi = i // 4, (i // 2) % 2, i % 2
        return copy(gtc.at[k, xi, yhi * 2 + yli], rs_buf.at[d - 1], rs_s.at[d - 1],
                    rs_r.at[d - 1], dev(xi, yli * 2 + k, yhi, z))

    def rs_go(d, _):
        rs_copy(d).start()
        return 0

    lax.fori_loop(1, 16, rs_go, 0)

    def lb_wait(d, acc):
        lb_copy(d).wait_recv()
        return acc + loss_b[d - 1]

    loss_src2[...] = lax.fori_loop(1, 16, lb_wait, loss_src[...])

    def la_copy(d):
        return copy(loss_src2, loss_a.at[d - 1], la_s.at[d - 1], la_r.at[d - 1],
                    (b, lax.rem(a + d, 8)))

    def la_go(d, _):
        la_copy(d).start()
        return 0

    lax.fori_loop(1, 8, la_go, 0)

    def rs_wait(d, _):
        rs_copy(d).wait_recv()
        fb_src[...] = fb_src[...] + rs_buf[d - 1]
        return 0

    fb_src[...] = gtc[k, x, yh * 2 + yl]
    lax.fori_loop(1, 16, rs_wait, 0)
    fb_src[...] = fb_src[...] * student_scale

    def fb_to(i):
        return (x * 4 + z, i)

    def fb_copy(i):
        return copy(fb_src, fb_buf.at[j * 2 + yh], fb_s.at[i], fb_r.at[j * 2 + yh], fb_to(i))

    def is_self(i):
        return (j == z) & (i == a)

    def fb_go(i, _):
        @pl.when(jnp.logical_not(is_self(i)))
        def _():
            fb_copy(i).start()

        return 0

    lax.fori_loop(0, 8, fb_go, 0)

    @pl.when(j == z)
    def _():
        fb_buf[j * 2 + yh] = fb_src[...]

    acc = gsend[0]
    for d in (1, 3, 2):
        g_copy(d).wait_recv()
        acc = acc + grecv[d - 1]
    gi_out[...] = acc * student_scale

    def la_wait(d, acc):
        la_copy(d).wait_recv()
        return acc + loss_a[d - 1]

    loss_out[...] = lax.fori_loop(1, 8, la_wait, loss_src2[...]) * (1.0 / (2.0 * 8 * 4608))

    def fb_wait(s, _):
        mine = (z == j) & (s == j * 2 + yh)

        @pl.when(jnp.logical_not(mine))
        def _():
            copy(fb_src, fb_buf.at[s], fb_s.at[s], fb_r.at[s], sib).wait_recv()

        return 0

    lax.fori_loop(0, 8, fb_wait, 0)
    for s in range(8):
        syl_, sk_, syh_ = s // 4, (s // 2) % 2, s % 2
        g = syh_ * 2 + syl_
        gt_out[sk_ * HALF : (sk_ + 1) * HALF, g * 128 : (g + 1) * 128] = fb_buf[s]

    for m in range(2):
        for d in range(2):
            for h in range(2):
                img_send(m, d, h).wait_send()
            img_relay(m, d).wait_send()

        @pl.when(is_source)
        def _():
            for c in text_first(m):
                c.wait_send()

        for d in (1, 2, 3):
            text_x(m, d).wait_send()
            row_copy(m, d).wait_send()
        for d in range(4):
            text_sib(m, d).wait_send()

        def col_sent(d, _):
            col_copy(m, d).wait_send()
            return 0

        lax.fori_loop(1, 16, col_sent, 0)
    for n in range(NCH):
        tgt_copy(n).wait_send()
    for d in (1, 2, 3):
        g_copy(d).wait_send()
    gc.wait_send()

    def sent16(d, _):
        rs_copy(d).wait_send()
        lb_copy(d).wait_send()
        return 0

    lax.fori_loop(1, 16, sent16, 0)

    def sent8(d, _):
        la_copy(d).wait_send()
        return 0

    lax.fori_loop(1, 8, sent8, 0)

    def fb_sent(i, _):
        @pl.when(jnp.logical_not(is_self(i)))
        def _():
            fb_copy(i).wait_send()

        return 0

    lax.fori_loop(0, 8, fb_sent, 0)


def per_device(student_image, student_text, teacher_image, teacher_text):
    vm = pl.BlockSpec(memory_space=pltpu.VMEM)
    dma = pltpu.SemaphoreType.DMA
    V = pltpu.VMEM
    sw, twd = student_image.shape[2], teacher_image.shape[2]
    loss, gi, gt = pl.pallas_call(
        kernel,
        name="distill",
        out_shape=(
            jax.ShapeDtypeStruct((8, 128), F32),
            jax.ShapeDtypeStruct((ROWS, sw), F32),
            jax.ShapeDtypeStruct((ROWS, sw), F32),
        ),
        in_specs=[vm] * 4,
        out_specs=(vm, vm, vm),
        scratch_shapes=[
            V((4, ROWS, twd), BF16), V((4, ROWS, sw), BF16),
            V((4 * ROWS, twd), BF16), V((4 * ROWS, sw), BF16),
            V((4, NCH, ROWS, CH), F32), V((4, NCH, ROWS, CH), F32),
            V((4, NCH, ROWS, CH), F32), V((4, NCH, ROWS, CH), F32),
            V((4, NCH, ROWS, CH), BF16),
            V((NCH, ROWS, CH), F32), V((NCH, ROWS, CH), F32), V((NCH, ROWS, CH), BF16),
            V((4, ROWS, sw), F32), V((3, ROWS, sw), F32),
            V((NCH, CH, sw), F32), V((4, 4, HALF, 128), F32),
            V((15, HALF, 128), F32), V((HALF, 128), F32), V((8, HALF, 128), F32),
            V((2, 4, 4, HALF, 128), F32),
            V((384, 128), F32), V((2, 8, 384), F32), V((2, 3, 8, 384), F32),
            V((384, 128), F32), V((128, 384), F32),
            V((2, NCH, 8, CH), F32), V((2, 15, NCH, 8, CH), F32),
            V((NCH, 8, CH), F32), V((8, CH), F32),
            V((8, 128), F32), V((15, 8, 128), F32), V((8, 128), F32), V((7, 8, 128), F32),
            dma((2, 3, 2)), dma((2, 3, 2)),
            dma((2, 3)), dma((2,)), dma((2, 3)), dma((2, 3)), dma((2, 4)), dma((2, 4)),
            dma((2, 3)), dma((2, 3)), dma((2, 15)), dma((2, 15)),
            dma((3,)), dma((3,)), dma((3,)), dma((3,)), dma((1,)), dma((1,)),
            dma((15,)), dma((15,)), dma((8,)), dma((8,)),
            dma((15,)), dma((15,)), dma((7,)), dma((7,)),
        ],
        compiler_params=pltpu.CompilerParams(
            collective_id=0, has_side_effects=True, vmem_limit_bytes=60 * 1024 * 1024
        ),
        cost_estimate=pl.CostEstimate(
            flops=8 * 10**9, bytes_accessed=4 * 2**20, transcendentals=6 * 10**6
        ),
    )(student_image[0], student_text, teacher_image[0], teacher_text)
    return loss[0, 0], gi[None], gt


def solution(mesh):
    return jax.shard_map(
        per_device,
        mesh=mesh,
        in_specs=(
            P("aug", "batch", None),
            P("batch", None),
            P("aug", "batch", None),
            P("batch", None),
        ),
        out_specs=(P(), P("aug", "batch", None), P("batch", None)),
        check_vma=False,
    )
```

time: 594 us -> 149 us (0.25); the launches traced: 585 us -> 148 us
  waiting for transfers between devices: 330 us -> 0 us
  blocking collectives: 174 us -> 0 us
  Pallas kernels: 0 us -> 144 us
  matrix products: 47.7 us -> 0 us
  between operations: 17.5 us -> 0.64 us
  other arithmetic: 13.4 us -> 0 us
    psum x2 -> x0, waiting for transfers between devices: 193 us -> none  [the longest x1 118 us: per_device(): target_weights = (lax.psum(own_targets, 'aug') / views).astype(jnp.bfloat16)]
    pallas_call x0 -> x1, Pallas kernels: none -> 144 us  [per_device(): pl.pallas_call(kernel, name='distill', out_shape=(jax.ShapeDtypeStruct((8...]
    psum x2 -> x0, blocking collectives: 122 us -> none  [the longest x1 69.3 us: per_device(): loss = lax.psum(local_loss, ('batch', 'aug')) / (2.0 * views * pairs)]
    all_gather x2 -> x0, waiting for transfers between devices: 105 us -> none  [the longest x1 63.7 us: per_device(): lax.all_gather(teacher_text, 'batch', axis=0, tiled=True)]
    pmax x1 -> x0, blocking collectives: 51.3 us -> none  [per_device(): lax.pmax(teacher_top.astype(jnp.bfloat16), 'batch')]
    dot_general x6 -> x0, matrix products: 47.7 us -> none  [the longest x2 18.5 us: per_device(): jnp.einsum('rc,rk->ck', block, image_rows, preferred_element_type=jnp.flo...]
    reduce_scatter x1 -> x0, waiting for transfers between devices: 31.3 us -> none  [per_device(): lax.psum_scatter((own_term - jnp.einsum('rc,rk->ck', block, image_rows, p...]
    reduce_sum x3 -> x0, other arithmetic: 7.07 us -> none  [the longest x1 5.78 us: per_device(): jnp.sum(jnp.exp(student_logits - student_high[None, :]), axis=0)]
  transfers between devices with their start and end apart: 5 -> 0, of which waited for: 5 -> 0; matrix products, arithmetic and copies ran while one was open for 5% -> 0% of each run, Pallas kernels for 0% -> 0%
where the time goes in v1:
time: 149 us; the launch traced here: 148 us
  Pallas kernels  144 us (97%)
  local copies, waits for them, and re-layouts  3.98 us (3%)
    pallas_call x1, Pallas kernels, per_device(): pl.pallas_call(kernel, name='distill', out_shape=(jax.ShapeDtypeStruct((8...  144 us

profile of v1, /device:TPU:97, one launch (start us, length us, event | category | flops | bytes accessed | tf_op | source)
XLA Modules:
  0.0 148.5 jit_solution(15765376590394144193)
XLA Ops:
  0.6 143.9 %distill.1 = (f32[8,128]{1,0:T(8,128)}, f32[288,512]{1,0:T(8,128)}, f32[288,512]{1,0:T(8,128)}) custom-call(bf16[288,512]{1,0:T(8,128)(2,1)} %bitcast.6, bf16[288,512]{1,0:T(8,128)(2,1)} %stext.1, bf16[288,1280]{1,0:T(8,128)(2,1)} %bitcast.5, bf16[288,1280]{1,0:T(8,128)(2,1)} %ttext.1), custom_call_target="tpu_custom_call" | custom-call | flops 8000000000 | bytes 4194304 | tf_op jit(solution)/shard_map/distill/pallas_call | solution.py:541
  144.5 1.2 slice.3
  145.7 0.0 copy-start
  145.7 2.0 %copy.9 = f32[1,288,512]{2,1,0:T(8,128)} copy(f32[1,288,512]{2,1,0:T(8,128)} %bitcast.4) | data formatting | bytes 1179648
  147.7 0.0 copy-done
  147.7 0.8 copy.10
Async XLA Ops:
  145.7 2.0 %copy-start = (f32[288,512]{1,0:T(8,128)S(1)}, f32[288,512]{1,0:T(8,128)}, u32[]{:S(2)}) copy-start(f32[288,512]{1,0:T(8,128)} %get-tuple-element.14) | copy-start | bytes 1769476

commit v2 on v1

--- a/solution.py
+++ b/solution.py
@@ -13,7 +13,7 @@
 BF16 = jnp.bfloat16
 ROWS = 288
 HALF = ROWS // 2
-CH = 384
+COLS = 4 * ROWS
 NCH = 3
 NT = (((1,), (1,)), ((), ()))
 NN = (((1,), (0,)), ((), ()))
@@ -29,7 +29,7 @@
     loss_out, gi_out, gt_out,
     it, is_, tt, ts, pt, qt, ps, qs, w, tgt, tgt_in, tw,
     gsend, grecv, gtp, gt_sib, rs_buf, fb_src, fb_buf, gtc,
-    rowst, rowsend, rowrecv, rowfac, rowtmp, colst, colrecv, colfac, collse,
+    rowst, rowsend, rowrecv, rowfac, rowtmp, colst, colrecv, colfac,
     loss_src, loss_b, loss_src2, loss_a,
     zi_s, zi_r, t1_s, t1_r, t2_s, t2_r, t3_s, t3_r,
     row_s, row_r, col_s, col_r, tgt_s, tgt_r, g_s, g_r, gc_s, gc_r,
@@ -55,24 +55,33 @@
             src_ref=src, dst_ref=dst, send_sem=ss, recv_sem=rs, device_id=to, device_id_type=MESH
         )
 
+    sent = []
+
+    def start(c):
+        c.start()
+        sent.append(c.wait_send)
+
+    def start_all(lo, hi, make):
+        def go(i, _):
+            make(i).start()
+            return 0
+
+        def gone(i, _):
+            make(i).wait_send()
+            return 0
+
+        lax.fori_loop(lo, hi, go, 0)
+        sent.append(lambda: lax.fori_loop(lo, hi, gone, 0))
+
     barrier = pltpu.get_barrier_semaphore()
 
-    def greet_plane(d, _):
-        i = lax.rem(b * 2 + yh + d, 32)
-        pl.semaphore_signal(barrier, 1, device_id=(i // 2, (i % 2) * 4 + z), device_id_type=MESH)
-        return 0
-
-    lax.fori_loop(1, 32, greet_plane, 0)
-
-    def greet_line(d, _):
-        dz, i = d // 8 + 1, d % 8
-        pl.semaphore_signal(
-            barrier, 1, device_id=dev(x, i // 2, i % 2, lax.rem(z + dz, 4)), device_id_type=MESH
-        )
-        return 0
-
-    lax.fori_loop(0, 24, greet_line, 0)
-    pl.semaphore_wait(barrier, 55)
+    near = [(b, yh * 4 + lax.rem(z + d, 4)) for d in (1, 2, 3)]
+    near += [(lax.rem(x + d, 4) * 4 + j, a) for d in (1, 2, 3)]
+    near += [(x * 4 + lax.rem(j + d, 4), a) for d in (1, 2, 3)]
+    near += [(b, (1 - yh) * 4 + z)]
+    for peer in near:
+        pl.semaphore_signal(barrier, 1, device_id=peer, device_id_type=MESH)
+    pl.semaphore_wait(barrier, len(near))
 
     zm1, zp1, zp2 = lax.rem(z + 3, 4), lax.rem(z + 1, 4), lax.rem(z + 2, 4)
     own = (timg, simg)
@@ -104,16 +113,14 @@
         copy(ref, ref, zi_s.at[m, 2, d], zi_r.at[m, 2, d], znext(1)).wait_recv()
 
     def img_start(m):
-        img_send(m, 0, 0).start()
-        img_send(m, 1, 1).start()
-        img_send(m, 0, 1).start()
-        img_send(m, 1, 0).start()
+        for d, h in ((0, 0), (1, 1), (0, 1), (1, 0)):
+            start(img_send(m, d, h))
 
     def img_pass_on(m):
         img_recv(m, 0, 0)
-        img_relay(m, 0).start()
+        start(img_relay(m, 0))
         img_recv(m, 1, 1)
-        img_relay(m, 1).start()
+        start(img_relay(m, 1))
 
     syl, sk = z // 2, z % 2
     is_source = j == z
@@ -138,6 +145,14 @@
                 c.start()
             tslab(m, x, k)[...] = own_text[m][pl.ds(k * HALF, HALF)]
 
+        def gone():
+            @pl.when(is_source)
+            def _():
+                for c in text_first(m):
+                    c.wait_send()
+
+        sent.append(gone)
+
     def text_x(m, d):
         return copy(tslab(m, x, k), tslab(m, x, k), t2_s.at[m, d - 1], t2_r.at[m, d - 1],
                     (lax.rem(x + d, 4) * 4 + j, a))
@@ -152,15 +167,15 @@
             copy(tslab(m, x, k), tslab(m, x, k), t1_s.at[m, 0], t1_r.at[m], sib).wait_recv()
 
         for d in (1, 3, 2):
-            text_x(m, d).start()
-        text_sib(m, 0).start()
+            start(text_x(m, d))
+        start(text_sib(m, 0))
 
     def text_share(m):
         for d in (1, 3, 2):
             blk = lax.rem(x + 4 - d, 4)
             copy(tslab(m, blk, k), tslab(m, blk, k), t2_s.at[m, d - 1], t2_r.at[m, d - 1],
                  sib).wait_recv()
-            text_sib(m, d).start()
+            start(text_sib(m, d))
 
     def text_wait(m):
         for d in range(4):
@@ -170,29 +185,20 @@
 
     lane = lax.broadcasted_iota(jnp.int32, (ROWS, 128), 1)
 
+    def fold(op, t):
+        return functools.reduce(op, [t[:, i * 128 : (i + 1) * 128] for i in range(COLS // 128)])
+
     def scores(m, v, pr, qr, scale):
-        def first(n, top):
-            t = dot(imgs[m][v], texts[m][pl.ds(n * CH, CH), :], NT) * scale
-            cm = jnp.max(t, axis=0, keepdims=True)
-            q = jnp.exp(t - cm)
-            pr[v, n] = t
-            qr[v, n] = q
-            colst[m, n, pl.ds(v, 1), :] = cm
-            colst[m, n, pl.ds(v + 4, 1), :] = jnp.sum(q, axis=0, keepdims=True)
-            return jnp.maximum(
-                top, jnp.maximum(jnp.maximum(t[:, :128], t[:, 128:256]), t[:, 256:])
-            )
-
-        top = lax.fori_loop(0, NCH, first, jnp.full((ROWS, 128), -jnp.inf, F32))
-        top = jnp.max(top, axis=1, keepdims=True)
-
-        def second(n, total):
-            p = jnp.exp(pr[v, n] - top)
-            pr[v, n] = p
-            return total + (p[:, :128] + p[:, 128:256] + p[:, 256:])
-
-        total = lax.fori_loop(0, NCH, second, jnp.zeros((ROWS, 128), F32))
-        total = jnp.sum(total, axis=1, keepdims=True)
+        t = dot(imgs[m][v], texts[m][...], NT) * scale
+        cm = jnp.max(t, axis=0, keepdims=True)
+        top = jnp.max(fold(jnp.maximum, t), axis=1, keepdims=True)
+        q = jnp.exp(t - cm)
+        qr[v] = q
+        p = jnp.exp(t - top)
+        pr[v] = p
+        colst[m, pl.ds(v, 1), :] = cm
+        colst[m, pl.ds(v + 4, 1), :] = jnp.sum(q, axis=0, keepdims=True)
+        total = jnp.sum(fold(jnp.add, p), axis=1, keepdims=True)
         rowst[:ROWS, :] = jnp.where(
             lane == v, top, jnp.where(lane == v + 4, total, rowst[:ROWS, :])
         )
@@ -206,14 +212,10 @@
                     (lax.rem(b + d, 16), a))
 
     def stats_start(m):
-        def go(d, _):
-            col_copy(m, d).start()
-            return 0
-
-        lax.fori_loop(1, 16, go, 0)
+        start_all(1, 16, lambda d: col_copy(m, d))
         rowsend[m] = jnp.transpose(rowst[...])[:8]
         for d in (1, 3, 2):
-            row_copy(m, d).start()
+            start(row_copy(m, d))
 
     def stats_finish(m):
         for d in (1, 3, 2):
@@ -238,19 +240,19 @@
         cmine = colst[m]
 
         def highest(d, t):
-            return jnp.maximum(t, colrecv[m, d, :, :4, :])
-
-        ctop = lax.fori_loop(0, 15, highest, cmine[:, :4, :])
+            return jnp.maximum(t, colrecv[m, d, :4, :])
+
+        ctop = lax.fori_loop(0, 15, highest, cmine[:4])
 
         def add(d, t):
             got = colrecv[m, d]
-            return t + got[:, 4:, :] * jnp.exp(got[:, :4, :] - ctop)
+            return t + got[4:] * jnp.exp(got[:4] - ctop)
 
         ctotal = lax.fori_loop(
-            0, 15, add, cmine[:, 4:, :] * jnp.exp(cmine[:, :4, :] - ctop)
+            0, 15, add, cmine[4:] * jnp.exp(cmine[:4] - ctop)
         )
         col_lse = ctop + jnp.log(ctotal)
-        colfac[:, 0:4, :] = jnp.exp(cmine[:, :4, :] - col_lse)
+        colfac[0:4, :] = jnp.exp(cmine[:4] - col_lse)
         return row_lse, col_lse
 
     rowst[...] = jnp.ones_like(rowst)
@@ -289,12 +291,13 @@
         return copy(tgt.at[n], tgt_in.at[n], tgt_s.at[n], tgt_r.at[n], partner)
 
     for n in range(NCH):
+        rows = slice(n * 96, (n + 1) * 96)
         acc = None
         for v in range(4):
-            term = pt[v, n] * rowfac[:ROWS, v : v + 1] + qt[v, n] * colfac[n, v : v + 1, :]
+            term = pt[v, rows] * rowfac[rows, v : v + 1] + qt[v, rows] * colfac[v : v + 1, :]
             acc = term if acc is None else acc + term
         tgt[n] = acc
-        tgt_copy(n).start()
+        start(tgt_copy(n))
 
     text_wait(1)
     scores(1, z, ps, qs, student_scale)
@@ -307,39 +310,32 @@
     scores(1, zp2, ps, qs, student_scale)
     stats_start(1)
     row_lse, col_lse = stats_finish(1)
-    rl = lax.broadcasted_iota(jnp.int32, (4, CH), 0)
-    cl = lax.broadcasted_iota(jnp.int32, (4, CH), 1)
-    lse_part = jnp.sum(
-        jnp.where((rl == z) & (cl < ROWS), row_lse, 0.0)
-        + jnp.sum(col_lse, axis=0) * (1.0 / 16.0),
-        axis=0, keepdims=True,
+    rl = lax.broadcasted_iota(jnp.int32, (4, 384), 0)
+    cl = lax.broadcasted_iota(jnp.int32, (4, 384), 1)
+    row_part = jnp.sum(jnp.where((rl == z) & (cl < ROWS), row_lse, 0.0), axis=0, keepdims=True)
+    lse_part = (
+        jnp.sum(row_part, axis=1, keepdims=True)
+        + jnp.sum(jnp.sum(col_lse, axis=0, keepdims=True), axis=1, keepdims=True) * (1.0 / 16.0)
     )
-    collse[0:1, :] = lse_part
 
     for v in range(4):
         for n in range(NCH):
-            w[v, n] = (
-                ps[v, n] * rowfac[:ROWS, v : v + 1] + qs[v, n] * colfac[n, v : v + 1, :]
+            rows = slice(n * 96, (n + 1) * 96)
+            w[v, rows] = (
+                ps[v, rows] * rowfac[rows, v : v + 1] + qs[v, rows] * colfac[v : v + 1, :]
             ).astype(BF16)
 
     def image_term(i, _):
         v = view_at(i)
-        acc = dot(w[v, 0], ts[0:CH, :], NN)
-        for n in range(1, NCH):
-            acc = acc + dot(w[v, n], ts[n * CH : (n + 1) * CH, :], NN)
-        gsend[i] = acc
+        gsend[i] = dot(w[v], ts[...], NN)
         return 0
 
     lax.fori_loop(0, 4, image_term, 0)
 
-    def text_term(n, _):
-        acc = dot(w[0, n], is_[0], TN)
-        for v in range(1, 4):
-            acc = acc + dot(w[v, n], is_[v], TN)
-        gtp[n] = acc
-        return 0
-
-    lax.fori_loop(0, NCH, text_term, 0)
+    acc = dot(w[0], is_[0], TN)
+    for v in range(1, 4):
+        acc = acc + dot(w[v], is_[v], TN)
+    gtp[...] = acc
     total_img = (
         is_[0].astype(F32) + is_[1].astype(F32) + is_[2].astype(F32) + is_[3].astype(F32)
     )
@@ -348,47 +344,36 @@
 
     for n in range(NCH):
         tgt_copy(n).wait_recv()
-        tw[n] = ((tgt[n] + tgt_in[n]) * 0.125).astype(BF16)
-    target_text = dot(tw[0], ts[0:CH, :], NN)
-    for n in range(1, NCH):
-        target_text = target_text + dot(tw[n], ts[n * CH : (n + 1) * CH, :], NN)
+        tw[n * 96 : (n + 1) * 96] = ((tgt[n] + tgt_in[n]) * 0.125).astype(BF16)
+    target_text = dot(tw[...], ts[...], NN)
 
     def g_copy(d):
         return copy(gsend.at[d], grecv.at[d - 1], g_s.at[d - 1], g_r.at[d - 1], znext(d))
 
     for d in (2, 1, 3):
         gsend[d] = gsend[d] - target_text
-        g_copy(d).start()
+        start(g_copy(d))
     gsend[0] = gsend[0] - target_text
 
-    for n in range(NCH):
-        res = gtp[n] - dot(tw[n], hi, TN) - dot(tw[n], lo, TN)
-        for s in range(8):
-            row = n * CH + s * 48
-            blk, inner = row // ROWS, row % ROWS
-            kk, off = inner // HALF, inner % HALF
-            for g in range(4):
-                gtc[kk, blk, g, off : off + 48, :] = res[
-                    s * 48 : (s + 1) * 48, g * 128 : (g + 1) * 128
-                ]
+    res = gtp[...] - dot(tw[...], hi, TN) - dot(tw[...], lo, TN)
+    for s in range(8):
+        row = s * HALF
+        for g in range(4):
+            gtc[s % 2, s // 2, g] = res[row : row + HALF, g * 128 : (g + 1) * 128]
     gc = copy(gtc.at[1 - k], gt_sib, gc_s.at[0], gc_r.at[0], sib)
-    gc.start()
+    start(gc)
 
     target_loss = jnp.sum(
         jnp.sum(total_img * target_text, axis=0, keepdims=True), axis=1, keepdims=True
     )
-    part = jnp.sum(collse[0:1, :], axis=1, keepdims=True) - target_loss * student_scale
+    part = lse_part - target_loss * student_scale
     loss_src[...] = jnp.broadcast_to(part, (8, 128))
 
     def lb_copy(d):
         return copy(loss_src, loss_b.at[d - 1], lb_s.at[d - 1], lb_r.at[d - 1],
                     (lax.rem(b + d, 16), a))
 
-    def lb_go(d, _):
-        lb_copy(d).start()
-        return 0
-
-    lax.fori_loop(1, 16, lb_go, 0)
+    start_all(1, 16, lb_copy)
 
     gc.wait_recv()
     for blk in range(4):
@@ -402,11 +387,7 @@
         return copy(gtc.at[k, xi, yhi * 2 + yli], rs_buf.at[d - 1], rs_s.at[d - 1],
                     rs_r.at[d - 1], dev(xi, yli * 2 + k, yhi, z))
 
-    def rs_go(d, _):
-        rs_copy(d).start()
-        return 0
-
-    lax.fori_loop(1, 16, rs_go, 0)
+    start_all(1, 16, rs_copy)
 
     def lb_wait(d, acc):
         lb_copy(d).wait_recv()
@@ -418,11 +399,7 @@
         return copy(loss_src2, loss_a.at[d - 1], la_s.at[d - 1], la_r.at[d - 1],
                     (b, lax.rem(a + d, 8)))
 
-    def la_go(d, _):
-        la_copy(d).start()
-        return 0
-
-    lax.fori_loop(1, 8, la_go, 0)
+    start_all(1, 8, la_copy)
 
     def rs_wait(d, _):
         rs_copy(d).wait_recv()
@@ -450,6 +427,15 @@
         return 0
 
     lax.fori_loop(0, 8, fb_go, 0)
+
+    def fb_gone(i, _):
+        @pl.when(jnp.logical_not(is_self(i)))
+        def _():
+            fb_copy(i).wait_send()
+
+        return 0
+
+    sent.append(lambda: lax.fori_loop(0, 8, fb_gone, 0))
 
     @pl.when(j == z)
     def _():
@@ -482,55 +468,8 @@
         g = syh_ * 2 + syl_
         gt_out[sk_ * HALF : (sk_ + 1) * HALF, g * 128 : (g + 1) * 128] = fb_buf[s]
 
-    for m in range(2):
-        for d in range(2):
-            for h in range(2):
-                img_send(m, d, h).wait_send()
-            img_relay(m, d).wait_send()
-
-        @pl.when(is_source)
-        def _():
-            for c in text_first(m):
-                c.wait_send()
-
-        for d in (1, 2, 3):
-            text_x(m, d).wait_send()
-            row_copy(m, d).wait_send()
-        for d in range(4):
-            text_sib(m, d).wait_send()
-
-        def col_sent(d, _):
-            col_copy(m, d).wait_send()
-            return 0
-
-        lax.fori_loop(1, 16, col_sent, 0)
-    for n in range(NCH):
-        tgt_copy(n).wait_send()
-    for d in (1, 2, 3):
-        g_copy(d).wait_send()
-    gc.wait_send()
-
-    def sent16(d, _):
-        rs_copy(d).wait_send()
-        lb_copy(d).wait_send()
-        return 0
-
-    lax.fori_loop(1, 16, sent16, 0)
-
-    def sent8(d, _):
-        la_copy(d).wait_send()
-        return 0
-
-    lax.fori_loop(1, 8, sent8, 0)
-
-    def fb_sent(i, _):
-        @pl.when(jnp.logical_not(is_self(i)))
-        def _():
-            fb_copy(i).wait_send()
-
-        return 0
-
-    lax.fori_loop(0, 8, fb_sent, 0)
+    for gone in sent:
+        gone()
 
 
 def per_device(student_image, student_text, teacher_image, teacher_text):
@@ -551,18 +490,17 @@
         scratch_shapes=[
             V((4, ROWS, twd), BF16), V((4, ROWS, sw), BF16),
             V((4 * ROWS, twd), BF16), V((4 * ROWS, sw), BF16),
-            V((4, NCH, ROWS, CH), F32), V((4, NCH, ROWS, CH), F32),
-            V((4, NCH, ROWS, CH), F32), V((4, NCH, ROWS, CH), F32),
-            V((4, NCH, ROWS, CH), BF16),
-            V((NCH, ROWS, CH), F32), V((NCH, ROWS, CH), F32), V((NCH, ROWS, CH), BF16),
+            V((4, ROWS, COLS), F32), V((4, ROWS, COLS), F32),
+            V((4, ROWS, COLS), F32), V((4, ROWS, COLS), F32),
+            V((4, ROWS, COLS), BF16),
+            V((NCH, 96, COLS), F32), V((NCH, 96, COLS), F32), V((ROWS, COLS), BF16),
             V((4, ROWS, sw), F32), V((3, ROWS, sw), F32),
-            V((NCH, CH, sw), F32), V((4, 4, HALF, 128), F32),
+            V((COLS, sw), F32), V((4, 4, HALF, 128), F32),
             V((15, HALF, 128), F32), V((HALF, 128), F32), V((8, HALF, 128), F32),
             V((2, 4, 4, HALF, 128), F32),
             V((384, 128), F32), V((2, 8, 384), F32), V((2, 3, 8, 384), F32),
             V((384, 128), F32), V((128, 384), F32),
-            V((2, NCH, 8, CH), F32), V((2, 15, NCH, 8, CH), F32),
-            V((NCH, 8, CH), F32), V((8, CH), F32),
+            V((2, 8, COLS), F32), V((2, 15, 8, COLS), F32), V((8, COLS), F32),
             V((8, 128), F32), V((15, 8, 128), F32), V((8, 128), F32), V((7, 8, 128), F32),
             dma((2, 3, 2)), dma((2, 3, 2)),
             dma((2, 3)), dma((2,)), dma((2, 3)), dma((2, 3)), dma((2, 4)), dma((2, 4)),

time: 149 us -> 143 us (0.960)
  Pallas kernels: 144 us -> 136 us
    pallas_call x1, Pallas kernels: 144 us -> 136 us  [per_device(): pl.pallas_call(kernel, name='distill', out_shape=(jax.ShapeDtypeStruct((8...]
where the time goes in v2:
time: 143 us; the launch traced here: 141 us
  Pallas kernels  136 us (95%)
  local copies, waits for them, and re-layouts  3.98 us (3%)
    pallas_call x1, Pallas kernels, per_device(): pl.pallas_call(kernel, name='distill', out_shape=(jax.ShapeDtypeStruct((8...  136 us

profile of v2, /device:TPU:97, one launch (start us, length us, event | category | flops | bytes accessed | tf_op | source)
XLA Modules:
  0.0 141.0 jit_solution(8578652457947499355)
XLA Ops:
  0.6 136.4 %distill.1 = (f32[8,128]{1,0:T(8,128)}, f32[288,512]{1,0:T(8,128)}, f32[288,512]{1,0:T(8,128)}) custom-call(bf16[288,512]{1,0:T(8,128)(2,1)} %bitcast.6, bf16[288,512]{1,0:T(8,128)(2,1)} %stext.1, bf16[288,1280]{1,0:T(8,128)(2,1)} %bitcast.5, bf16[288,1280]{1,0:T(8,128)(2,1)} %ttext.1), custom_call_target="tpu_custom_call" | custom-call | flops 8000000000 | bytes 4194304 | tf_op jit(solution)/shard_map/distill/pallas_call | solution.py:480
  137.0 1.2 slice.3
  138.2 0.0 copy-start
  138.2 2.0 %copy.9 = f32[1,288,512]{2,1,0:T(8,128)} copy(f32[1,288,512]{2,1,0:T(8,128)} %bitcast.4) | data formatting | bytes 1179648
  140.2 0.0 copy-done
  140.2 0.8 copy.10
Async XLA Ops:
  138.2 2.0 %copy-start = (f32[288,512]{1,0:T(8,128)S(1)}, f32[288,512]{1,0:T(8,128)}, u32[]{:S(2)}) copy-start(f32[288,512]{1,0:T(8,128)} %get-tuple-element.14) | copy-start | bytes 1769476

commit v3 on v2

--- a/solution.py
+++ b/solution.py
@@ -27,12 +27,14 @@
 def kernel(
     simg, stext, timg, ttext,
     loss_out, gi_out, gt_out,
-    it, is_, tt, ts, pt, qt, ps, qs, w, tgt, tgt_in, tw,
-    gsend, grecv, gtp, gt_sib, rs_buf, fb_src, fb_buf, gtc,
-    rowst, rowsend, rowrecv, rowfac, rowtmp, colst, colrecv, colfac,
+    it, is_, tt, ts, pt, qt, ps, qs, w, tgt, tgt_mine, tgt_in, tw,
+    isum, isum_in, isum8, hi, lo, tt_part, tt_in, tt_src, tt_all,
+    gsend, grecv, gfar_in, gtp, gt_sib, ra_in, rb_in, ra_sum, rb_sum, ra2_in, rb2_in, fb_src, fb_buf, gtc,
+    rowst, rowsend, rowrecv, rowfac, rowtmp, colst, quad_in, colq, colx_in, colfac,
     loss_src, loss_b, loss_src2, loss_a,
-    zi_s, zi_r, t1_s, t1_r, t2_s, t2_r, t3_s, t3_r,
-    row_s, row_r, col_s, col_r, tgt_s, tgt_r, g_s, g_r, gc_s, gc_r,
+    zi_s, zi_r, t1_s, t1_r, t2_s, t2_r, t3_s, t3_r, t4_s, t4_r,
+    iy_s, iy_r, iz_s, iz_r, tz_s, tz_r, ta_s, ta_r,
+    quad_s, quad_r, row_s, row_r, col_s, col_r, tgt_s, tgt_r, g_s, g_r, gc_s, gc_r,
     rs_s, rs_r, fb_s, fb_r, lb_s, lb_r, la_s, la_r,
 ):
     b = lax.axis_index("batch")
@@ -78,7 +80,7 @@
     near = [(b, yh * 4 + lax.rem(z + d, 4)) for d in (1, 2, 3)]
     near += [(lax.rem(x + d, 4) * 4 + j, a) for d in (1, 2, 3)]
     near += [(x * 4 + lax.rem(j + d, 4), a) for d in (1, 2, 3)]
-    near += [(b, (1 - yh) * 4 + z)]
+    near += [(x * 4 + lax.rem(j + d, 4), (1 - yh) * 4 + z) for d in range(4)]
     for peer in near:
         pl.semaphore_signal(barrier, 1, device_id=peer, device_id_type=MESH)
     pl.semaphore_wait(barrier, len(near))
@@ -135,7 +137,7 @@
             copy(own_text[m].at[half(0)], tslab(m, x, 0),
                  t1_s.at[m, 1], t1_r.at[m], dev(x, (1 - syl) * 2, yh, z)),
             copy(own_text[m].at[half(1)], tslab(m, x, 1),
-                 t1_s.at[m, 2], t1_r.at[m], dev(x, (1 - syl) * 2 + 1, yh, z)),
+                 t1_s.at[m, 2], t1_r.at[m], dev(x, (1 - syl) * 2 + 1, 1 - yh, z)),
         )
 
     def text_start(m):
@@ -157,6 +159,18 @@
         return copy(tslab(m, x, k), tslab(m, x, k), t2_s.at[m, d - 1], t2_r.at[m, d - 1],
                     (lax.rem(x + d, 4) * 4 + j, a))
 
+    def text_got(m, d):
+        slab = tslab(m, lax.rem(x + 4 - d, 4), k)
+        copy(slab, slab, t2_s.at[m, d - 1], t2_r.at[m, d - 1], sib).wait_recv()
+
+    def tlanes(m, blk, i):
+        width = texts[m].shape[1] // 2
+        return texts[m].at[pl.ds(blk * ROWS + k * HALF, HALF), i * width : (i + 1) * width]
+
+    def text_relay(m, i):
+        ref = tlanes(m, lax.rem(x + 3 - 2 * i, 4), i)
+        return copy(ref, ref, t4_s.at[m, i], t4_r.at[m, i], (lax.rem(x + 1 + 2 * i, 4) * 4 + j, a))
+
     def text_sib(m, d):
         blk = lax.rem(x + 4 - d, 4)
         return copy(tslab(m, blk, k), tslab(m, blk, k), t3_s.at[m, d], t3_r.at[m, d], sib)
@@ -166,16 +180,21 @@
         def _():
             copy(tslab(m, x, k), tslab(m, x, k), t1_s.at[m, 0], t1_r.at[m], sib).wait_recv()
 
-        for d in (1, 3, 2):
+        for d in (1, 3):
             start(text_x(m, d))
         start(text_sib(m, 0))
 
-    def text_share(m):
-        for d in (1, 3, 2):
-            blk = lax.rem(x + 4 - d, 4)
-            copy(tslab(m, blk, k), tslab(m, blk, k), t2_s.at[m, d - 1], t2_r.at[m, d - 1],
-                 sib).wait_recv()
+    def text_pass_on(m):
+        for d in (1, 3):
+            text_got(m, d)
+            start(text_relay(m, d // 2))
             start(text_sib(m, d))
+
+    def text_far(m):
+        for i in range(2):
+            ref = tlanes(m, lax.rem(x + 2, 4), i)
+            copy(ref, ref, t4_s.at[m, i], t4_r.at[m, i], sib).wait_recv()
+        start(text_sib(m, 2))
 
     def text_wait(m):
         for d in range(4):
@@ -207,99 +226,67 @@
         return copy(rowsend.at[m], rowrecv.at[m, d - 1], row_s.at[m, d - 1], row_r.at[m, d - 1],
                     znext(d))
 
+    def quad_copy(m, d):
+        return copy(colst.at[m], quad_in.at[m, d - 1], quad_s.at[m, d - 1], quad_r.at[m, d - 1],
+                    (x * 4 + lax.rem(j + d, 4), a))
+
     def col_copy(m, d):
-        return copy(colst.at[m], colrecv.at[m, d - 1], col_s.at[m, d - 1], col_r.at[m, d - 1],
-                    (lax.rem(b + d, 16), a))
+        return copy(colq.at[m], colx_in.at[m, d - 1], col_s.at[m, d - 1], col_r.at[m, d - 1],
+                    (lax.rem(x + d, 4) * 4 + j, a))
+
+    def merged(mine, others):
+        top = functools.reduce(jnp.maximum, [t[:4] for t in others], mine[:4])
+        total = mine[4:] * jnp.exp(mine[:4] - top)
+        for t in others:
+            total = total + t[4:] * jnp.exp(t[:4] - top)
+        return top, total
 
     def stats_start(m):
-        start_all(1, 16, lambda d: col_copy(m, d))
+        for d in (1, 2, 3):
+            start(quad_copy(m, d))
         rowsend[m] = jnp.transpose(rowst[...])[:8]
         for d in (1, 3, 2):
             start(row_copy(m, d))
+
+    def stats_middle(m):
+        for d in (1, 2, 3):
+            quad_copy(m, d).wait_recv()
+        top, total = merged(colst[m], [quad_in[m, d] for d in range(3)])
+        colq[m, 0:4, :] = top
+        colq[m, 4:8, :] = total
+        for d in (1, 3, 2):
+            start(col_copy(m, d))
 
     def stats_finish(m):
         for d in (1, 3, 2):
             row_copy(m, d).wait_recv()
         mine = rowsend[m]
-        top = mine[:4]
-        for d in range(3):
-            top = jnp.maximum(top, rowrecv[m, d, :4])
-        total = mine[4:] * jnp.exp(mine[:4] - top)
-        for d in range(3):
-            got = rowrecv[m, d]
-            total = total + got[4:] * jnp.exp(got[:4] - top)
+        top, total = merged(mine, [rowrecv[m, d] for d in range(3)])
         row_lse = top + jnp.log(total)
         rowtmp[0:4, :] = jnp.exp(mine[:4] - row_lse)
-        rowfac[...] = jnp.transpose(rowtmp[...])
-
-        def arrived(d, _):
+        rowfac[m] = jnp.transpose(rowtmp[...])
+        for d in (1, 3, 2):
             col_copy(m, d).wait_recv()
-            return 0
-
-        lax.fori_loop(1, 16, arrived, 0)
-        cmine = colst[m]
-
-        def highest(d, t):
-            return jnp.maximum(t, colrecv[m, d, :4, :])
-
-        ctop = lax.fori_loop(0, 15, highest, cmine[:4])
-
-        def add(d, t):
-            got = colrecv[m, d]
-            return t + got[4:] * jnp.exp(got[:4] - ctop)
-
-        ctotal = lax.fori_loop(
-            0, 15, add, cmine[4:] * jnp.exp(cmine[:4] - ctop)
-        )
-        col_lse = ctop + jnp.log(ctotal)
-        colfac[0:4, :] = jnp.exp(cmine[:4] - col_lse)
+        top, total = merged(colq[m], [colx_in[m, d] for d in range(3)])
+        col_lse = top + jnp.log(total)
+        colfac[m, 0:4, :] = jnp.exp(colst[m, 0:4, :] - col_lse)
         return row_lse, col_lse
 
     rowst[...] = jnp.ones_like(rowst)
     rowtmp[...] = jnp.zeros_like(rowtmp)
+    img_start(1)
+    text_start(1)
+    text_start(0)
+    is_[z] = simg[...]
+    it[z] = timg[...]
+    text_spread(1)
+    img_pass_on(1)
     img_start(0)
-    text_start(0)
-    it[z] = timg[...]
-    is_[z] = simg[...]
+    text_pass_on(1)
     text_spread(0)
-    img_pass_on(0)
-    text_start(1)
-    img_start(1)
-    text_share(0)
-    text_spread(1)
-    text_wait(0)
-
-    def view_at(i):
-        return lax.rem(z + i, 4)
-
-    scores(0, z, pt, qt, teacher_scale)
-    img_pass_on(1)
-    img_recv(0, 0, 1)
-    scores(0, zm1, pt, qt, teacher_scale)
-    img_recv(0, 1, 0)
-    scores(0, zp1, pt, qt, teacher_scale)
-    text_share(1)
-    img_recv_far(0, 0)
-    img_recv_far(0, 1)
-    scores(0, zp2, pt, qt, teacher_scale)
-    stats_start(0)
-    stats_finish(0)
-
-    partner = (b, (1 - yh) * 4 + z)
-
-    def tgt_copy(n):
-        return copy(tgt.at[n], tgt_in.at[n], tgt_s.at[n], tgt_r.at[n], partner)
-
-    for n in range(NCH):
-        rows = slice(n * 96, (n + 1) * 96)
-        acc = None
-        for v in range(4):
-            term = pt[v, rows] * rowfac[rows, v : v + 1] + qt[v, rows] * colfac[v : v + 1, :]
-            acc = term if acc is None else acc + term
-        tgt[n] = acc
-        start(tgt_copy(n))
-
+    text_far(1)
     text_wait(1)
+
     scores(1, z, ps, qs, student_scale)
     img_recv(1, 0, 1)
     scores(1, zm1, ps, qs, student_scale)
@@ -309,6 +296,43 @@
     img_recv_far(1, 1)
     scores(1, zp2, ps, qs, student_scale)
     stats_start(1)
+
+    partner = (b, (1 - yh) * 4 + z)
+    total_img = (
+        is_[0].astype(F32) + is_[1].astype(F32) + is_[2].astype(F32) + is_[3].astype(F32)
+    )
+    for g in range(4):
+        isum[0, g] = total_img[:HALF, g * 128 : (g + 1) * 128]
+        isum[1, g] = total_img[HALF:, g * 128 : (g + 1) * 128]
+    iy = copy(isum.at[1 - yh, z], isum_in.at[z], iy_s.at[0], iy_r.at[0], partner)
+    start(iy)
+    text_pass_on(0)
+    stats_middle(1)
+    img_pass_on(0)
+    text_far(0)
+    text_wait(0)
+    scores(0, z, pt, qt, teacher_scale)
+    img_recv(0, 0, 1)
+    scores(0, zm1, pt, qt, teacher_scale)
+    img_recv(0, 1, 0)
+    scores(0, zp1, pt, qt, teacher_scale)
+    img_recv_far(0, 0)
+    img_recv_far(0, 1)
+    scores(0, zp2, pt, qt, teacher_scale)
+    stats_start(0)
+
+    def iz_copy(d):
+        slot = isum_in.at[z]
+        return copy(slot, slot, iz_s.at[d - 1], iz_r.at[d - 1], znext(d))
+
+    def iz_wait(d):
+        slot = isum_in.at[lax.rem(z + 4 - d, 4)]
+        copy(slot, slot, iz_s.at[d - 1], iz_r.at[d - 1], partner).wait_recv()
+
+    iy.wait_recv()
+    for d in (1, 3, 2):
+        start(iz_copy(d))
+
     row_lse, col_lse = stats_finish(1)
     rl = lax.broadcasted_iota(jnp.int32, (4, 384), 0)
     cl = lax.broadcasted_iota(jnp.int32, (4, 384), 1)
@@ -318,44 +342,81 @@
         + jnp.sum(jnp.sum(col_lse, axis=0, keepdims=True), axis=1, keepdims=True) * (1.0 / 16.0)
     )
 
-    for v in range(4):
-        for n in range(NCH):
-            rows = slice(n * 96, (n + 1) * 96)
-            w[v, rows] = (
-                ps[v, rows] * rowfac[rows, v : v + 1] + qs[v, rows] * colfac[v : v + 1, :]
-            ).astype(BF16)
-
-    def image_term(i, _):
-        v = view_at(i)
-        gsend[i] = dot(w[v], ts[...], NN)
-        return 0
-
-    lax.fori_loop(0, 4, image_term, 0)
-
+    stats_middle(0)
+
+    for d in (2, 1, 3, 0):
+        v = lax.rem(z + d, 4)
+        factor = jnp.sum(jnp.where(lane == v, rowfac[1, :ROWS, :], 0.0), axis=1, keepdims=True)
+        w[v] = (ps[v] * factor + qs[v] * colfac[1, pl.ds(v, 1), :]).astype(BF16)
+        gsend[d] = dot(w[v], ts[...], NN)
+
+    def g_far(h):
+        return copy(gsend.at[2, half(h)], gfar_in.at[h], g_s.at[2, h], g_r.at[2, h],
+                    znext(1 if h == 0 else 3))
+
+    def g_copy(i, h):
+        d = 1 + 2 * i
+        return copy(gsend.at[d, half(h)], grecv.at[i, half(h)], g_s.at[i, h], g_r.at[i, h],
+                    znext(d))
+
+    start(g_far(0))
+    start(g_far(1))
+    start(g_copy(0, 1))
+    start(g_copy(1, 0))
+
+    stats_finish(0)
+
+
+    def tgt_copy(n):
+        return copy(tgt.at[n], tgt_in.at[n], tgt_s.at[n], tgt_r.at[n], partner)
+
+    def own_targets(h, n):
+        rows = pl.ds(pl.multiple_of(h * HALF + n * 48, 16), 48)
+        acc = None
+        for v in range(4):
+            term = pt[v, rows] * rowfac[0, rows, v : v + 1] + qt[v, rows] * colfac[0, v : v + 1, :]
+            acc = term if acc is None else acc + term
+        return acc
+
+    for n in range(NCH):
+        tgt[n] = own_targets(1 - yh, n)
+        start(tgt_copy(n))
     acc = dot(w[0], is_[0], TN)
     for v in range(1, 4):
         acc = acc + dot(w[v], is_[v], TN)
     gtp[...] = acc
-    total_img = (
-        is_[0].astype(F32) + is_[1].astype(F32) + is_[2].astype(F32) + is_[3].astype(F32)
-    )
-    hi = total_img.astype(BF16)
-    lo = (total_img - hi.astype(F32)).astype(BF16)
+    for n in range(NCH):
+        tgt_mine[n] = own_targets(yh, n)
+
+    for d in (1, 3, 2):
+        iz_wait(d)
+    for g in range(4):
+        isum8[g] = isum_in[g] + isum[yh, g]
+    for g in range(4):
+        t = isum8[g]
+        hi[:, g * 128 : (g + 1) * 128] = t.astype(BF16)
+        lo[:, g * 128 : (g + 1) * 128] = (t - t.astype(BF16).astype(F32)).astype(BF16)
+    for i in range(2):
+        g_far(i).wait_recv()
+        rows = slice(i * HALF, (i + 1) * HALF)
+        gsend[1 + 2 * i, rows] = gsend[1 + 2 * i, rows] + gfar_in[i]
+        start(g_copy(i, i))
 
     for n in range(NCH):
         tgt_copy(n).wait_recv()
-        tw[n * 96 : (n + 1) * 96] = ((tgt[n] + tgt_in[n]) * 0.125).astype(BF16)
+        tw[n * 48 : (n + 1) * 48] = ((tgt_mine[n] + tgt_in[n]) * 0.125).astype(BF16)
     target_text = dot(tw[...], ts[...], NN)
-
-    def g_copy(d):
-        return copy(gsend.at[d], grecv.at[d - 1], g_s.at[d - 1], g_r.at[d - 1], znext(d))
+    for g in range(4):
+        tt_part[g] = target_text[:, g * 128 : (g + 1) * 128]
+
+    def tz_copy(d):
+        return copy(tt_part.at[lax.rem(z + d, 4)], tt_in.at[d - 1], tz_s.at[d - 1],
+                    tz_r.at[d - 1], znext(d))
 
     for d in (2, 1, 3):
-        gsend[d] = gsend[d] - target_text
-        start(g_copy(d))
-    gsend[0] = gsend[0] - target_text
-
-    res = gtp[...] - dot(tw[...], hi, TN) - dot(tw[...], lo, TN)
+        start(tz_copy(d))
+
+    res = gtp[...] - dot(tw[...], hi[...], TN) - dot(tw[...], lo[...], TN)
     for s in range(8):
         row = s * HALF
         for g in range(4):
@@ -363,9 +424,10 @@
     gc = copy(gtc.at[1 - k], gt_sib, gc_s.at[0], gc_r.at[0], sib)
     start(gc)
 
-    target_loss = jnp.sum(
-        jnp.sum(total_img * target_text, axis=0, keepdims=True), axis=1, keepdims=True
-    )
+    target_loss = isum8[0] * tt_part[0]
+    for g in range(1, 4):
+        target_loss = target_loss + isum8[g] * tt_part[g]
+    target_loss = jnp.sum(jnp.sum(target_loss, axis=0, keepdims=True), axis=1, keepdims=True)
     part = lse_part - target_loss * student_scale
     loss_src[...] = jnp.broadcast_to(part, (8, 128))
 
@@ -379,15 +441,58 @@
     for blk in range(4):
         for g in range(4):
             gtc[k, blk, g] = gtc[k, blk, g] + gt_sib[blk, g]
-    chip = x * 4 + yl * 2 + yh
-
-    def rs_copy(d):
-        i = lax.rem(chip + d, 16)
-        xi, yli, yhi = i // 4, (i // 2) % 2, i % 2
-        return copy(gtc.at[k, xi, yhi * 2 + yli], rs_buf.at[d - 1], rs_s.at[d - 1],
-                    rs_r.at[d - 1], dev(xi, yli * 2 + k, yhi, z))
-
-    start_all(1, 16, rs_copy)
+    y = yh * 2 + yl
+    pieces = gtc.at[k]
+
+    def ydev(d):
+        yd = lax.rem(y + d, 4)
+        return dev(x, (yd % 2) * 2 + k, yd // 2, z)
+
+    def xdev(d):
+        return dev(lax.rem(x + d, 4), j, yh, z)
+
+    def ra_copy(d):
+        return copy(pieces.at[lax.rem(x + d, 4), :, 0:72, :], ra_in.at[d - 1],
+                    rs_s.at[0, d - 1], rs_r.at[0, d - 1], xdev(d))
+
+    def rb_copy(d):
+        return copy(pieces.at[:, lax.rem(y + d, 4), 72:144, :], rb_in.at[d - 1],
+                    rs_s.at[1, d - 1], rs_r.at[1, d - 1], ydev(d))
+
+    def ra2_copy(d):
+        return copy(ra_sum.at[lax.rem(y + d, 4)], ra2_in.at[d - 1],
+                    rs_s.at[2, d - 1], rs_r.at[2, d - 1], ydev(d))
+
+    def rb2_copy(d):
+        return copy(rb_sum.at[lax.rem(x + d, 4)], rb2_in.at[d - 1],
+                    rs_s.at[3, d - 1], rs_r.at[3, d - 1], xdev(d))
+
+    for d in (1, 3, 2):
+        start(ra_copy(d))
+        start(rb_copy(d))
+
+    total = tt_part[z]
+    for d in (1, 3, 2):
+        tz_copy(d).wait_recv()
+        total = total + tt_in[d - 1]
+    tt_src[...] = total
+
+    a_in = (1 - yh) * 4 + z
+    ty = copy(tt_src, tt_all.at[a], ta_s.at[0], ta_r.at[a], partner)
+    start(ty)
+
+    def ta_copy(d):
+        return copy(tt_src, tt_all.at[a], ta_s.at[d], ta_r.at[a], znext(d))
+
+    def tb_copy(d):
+        return copy(tt_all.at[a_in], tt_all.at[a_in], ta_s.at[3 + d], ta_r.at[a_in], znext(d))
+
+    def t_wait(slot):
+        copy(tt_src, tt_all.at[slot], ta_s.at[0], ta_r.at[slot], partner).wait_recv()
+
+    for d in (1, 3, 2):
+        start(ta_copy(d))
+    tt_all[a] = total
 
     def lb_wait(d, acc):
         lb_copy(d).wait_recv()
@@ -401,14 +506,30 @@
 
     start_all(1, 8, la_copy)
 
-    def rs_wait(d, _):
-        rs_copy(d).wait_recv()
-        fb_src[...] = fb_src[...] + rs_buf[d - 1]
-        return 0
-
-    fb_src[...] = gtc[k, x, yh * 2 + yl]
-    lax.fori_loop(1, 16, rs_wait, 0)
-    fb_src[...] = fb_src[...] * student_scale
+    ra_sum[...] = gtc[k, x, :, 0:72, :]
+    rb_sum[...] = gtc[k, :, y, 72:144, :]
+    for d in (1, 3, 2):
+        ra_copy(d).wait_recv()
+        ra_sum[...] = ra_sum[...] + ra_in[d - 1]
+    for d in (1, 3, 2):
+        start(ra2_copy(d))
+    for d in (1, 3, 2):
+        rb_copy(d).wait_recv()
+        rb_sum[...] = rb_sum[...] + rb_in[d - 1]
+    for d in (1, 3, 2):
+        start(rb2_copy(d))
+    t_wait(a_in)
+    for d in (1, 3, 2):
+        start(tb_copy(d))
+    first, last = ra_sum[y], rb_sum[x]
+    for d in (1, 3, 2):
+        ra2_copy(d).wait_recv()
+        first = first + ra2_in[d - 1]
+    for d in (1, 3, 2):
+        rb2_copy(d).wait_recv()
+        last = last + rb2_in[d - 1]
+    fb_src[0:72, :] = first * student_scale
+    fb_src[72:144, :] = last * student_scale
 
     def fb_to(i):
         return (x * 4 + z, i)
@@ -442,10 +563,20 @@
         fb_buf[j * 2 + yh] = fb_src[...]
 
     acc = gsend[0]
-    for d in (1, 3, 2):
-        g_copy(d).wait_recv()
-        acc = acc + grecv[d - 1]
-    gi_out[...] = acc * student_scale
+    for i in range(2):
+        g_copy(i, 0).wait_recv()
+        g_copy(i, 1).wait_recv()
+        acc = acc + grecv[i]
+
+    for d in (1, 3, 2):
+        zd = lax.rem(z + d, 4)
+        t_wait(yh * 4 + zd)
+        t_wait((1 - yh) * 4 + zd)
+    for h in range(2):
+        rows = slice(h * HALF, (h + 1) * HALF)
+        for g in range(4):
+            lanes = slice(g * 128, (g + 1) * 128)
+            gi_out[rows, lanes] = (acc[rows, lanes] - tt_all[h * 4 + g]) * student_scale
 
     def la_wait(d, acc):
         la_copy(d).wait_recv()
@@ -493,20 +624,30 @@
             V((4, ROWS, COLS), F32), V((4, ROWS, COLS), F32),
             V((4, ROWS, COLS), F32), V((4, ROWS, COLS), F32),
             V((4, ROWS, COLS), BF16),
-            V((NCH, 96, COLS), F32), V((NCH, 96, COLS), F32), V((ROWS, COLS), BF16),
-            V((4, ROWS, sw), F32), V((3, ROWS, sw), F32),
+            V((NCH, 48, COLS), F32), V((NCH, 48, COLS), F32), V((NCH, 48, COLS), F32),
+            V((HALF, COLS), BF16),
+            V((2, 4, HALF, 128), F32), V((4, HALF, 128), F32), V((4, HALF, 128), F32),
+            V((HALF, sw), BF16), V((HALF, sw), BF16),
+            V((4, HALF, 128), F32), V((3, HALF, 128), F32), V((HALF, 128), F32),
+            V((8, HALF, 128), F32),
+            V((4, ROWS, sw), F32), V((2, ROWS, sw), F32), V((2, HALF, sw), F32),
             V((COLS, sw), F32), V((4, 4, HALF, 128), F32),
-            V((15, HALF, 128), F32), V((HALF, 128), F32), V((8, HALF, 128), F32),
+            V((3, 4, 72, 128), F32), V((3, 4, 72, 128), F32), V((4, 72, 128), F32),
+            V((4, 72, 128), F32), V((3, 72, 128), F32), V((3, 72, 128), F32),
+            V((HALF, 128), F32), V((8, HALF, 128), F32),
             V((2, 4, 4, HALF, 128), F32),
             V((384, 128), F32), V((2, 8, 384), F32), V((2, 3, 8, 384), F32),
-            V((384, 128), F32), V((128, 384), F32),
-            V((2, 8, COLS), F32), V((2, 15, 8, COLS), F32), V((8, COLS), F32),
+            V((2, 384, 128), F32), V((128, 384), F32),
+            V((2, 8, COLS), F32), V((2, 3, 8, COLS), F32), V((2, 8, COLS), F32),
+            V((2, 3, 8, COLS), F32), V((2, 8, COLS), F32),
             V((8, 128), F32), V((15, 8, 128), F32), V((8, 128), F32), V((7, 8, 128), F32),
             dma((2, 3, 2)), dma((2, 3, 2)),
             dma((2, 3)), dma((2,)), dma((2, 3)), dma((2, 3)), dma((2, 4)), dma((2, 4)),
-            dma((2, 3)), dma((2, 3)), dma((2, 15)), dma((2, 15)),
-            dma((3,)), dma((3,)), dma((3,)), dma((3,)), dma((1,)), dma((1,)),
-            dma((15,)), dma((15,)), dma((8,)), dma((8,)),
+            dma((2, 2)), dma((2, 2)),
+            dma((1,)), dma((1,)), dma((3,)), dma((3,)), dma((3,)), dma((3,)), dma((7,)), dma((8,)),
+            dma((2, 3)), dma((2, 3)), dma((2, 3)), dma((2, 3)), dma((2, 3)), dma((2, 3)),
+            dma((3,)), dma((3,)), dma((3, 2)), dma((3, 2)), dma((1,)), dma((1,)),
+            dma((4, 3)), dma((4, 3)), dma((8,)), dma((8,)),
             dma((15,)), dma((15,)), dma((7,)), dma((7,)),
         ],
         compiler_params=pltpu.CompilerParams(

time: 143 us -> 115 us (0.80)
  Pallas kernels: 136 us -> 108 us
    pallas_call x1, Pallas kernels: 136 us -> 108 us  [per_device(): pl.pallas_call(kernel, name='distill', out_shape=(jax.ShapeDtypeStruct((8...]
where the time goes in v3:
time: 115 us; the launch traced here: 113 us
  Pallas kernels  108 us (94%)
  local copies, waits for them, and re-layouts  3.98 us (3%)
    pallas_call x1, Pallas kernels, per_device(): pl.pallas_call(kernel, name='distill', out_shape=(jax.ShapeDtypeStruct((8...  108 us
    unnamed x4, local copies, waits for them, and re-layouts  2.8 us

profile of v3, /device:TPU:97, one launch (start us, length us, event | category | flops | bytes accessed | tf_op | source)
XLA Modules:
  0.0 112.6 jit_solution(14941242251633478413)
XLA Ops:
  0.6 108.0 %distill.1 = (f32[8,128]{1,0:T(8,128)}, f32[288,512]{1,0:T(8,128)}, f32[288,512]{1,0:T(8,128)}) custom-call(bf16[288,512]{1,0:T(8,128)(2,1)} %bitcast.6, bf16[288,512]{1,0:T(8,128)(2,1)} %stext.1, bf16[288,1280]{1,0:T(8,128)(2,1)} %bitcast.5, bf16[288,1280]{1,0:T(8,128)(2,1)} %ttext.1), custom_call_target="tpu_custom_call" | custom-call | flops 8000000000 | bytes 4194304 | tf_op jit(solution)/shard_map/distill/pallas_call | solution.py:611
  108.6 1.2 %slice.3 = f32[1,1]{1,0:T(1,128)} slice(f32[8,128]{1,0:T(8,128)} %get-tuple-element.6), slice={[0:1], [0:1]} | slice | bytes 8 | tf_op jit(solution)/shard_map/slice | solution.py:660
  109.8 0.0 copy-start
  109.8 2.0 %copy.9 = f32[1,288,512]{2,1,0:T(8,128)} copy(f32[1,288,512]{2,1,0:T(8,128)} %bitcast.4) | data formatting | bytes 1179648
  111.8 0.0 copy-done
  111.8 0.8 copy.10
Async XLA Ops:
  109.8 2.0 %copy-start = (f32[288,512]{1,0:T(8,128)S(1)}, f32[288,512]{1,0:T(8,128)}, u32[]{:S(2)}) copy-start(f32[288,512]{1,0:T(8,128)} %get-tuple-element.14) | copy-start | bytes 1769476

commit v4 on v3

--- a/solution.py
+++ b/solution.py
@@ -26,7 +26,7 @@
 
 def kernel(
     simg, stext, timg, ttext,
-    loss_out, gi_out, gt_out,
+    loss_out, grads_out,
     it, is_, tt, ts, pt, qt, ps, qs, w, tgt, tgt_mine, tgt_in, tw,
     isum, isum_in, isum8, hi, lo, tt_part, tt_in, tt_src, tt_all,
     gsend, grecv, gfar_in, gtp, gt_sib, ra_in, rb_in, ra_sum, rb_sum, ra2_in, rb2_in, fb_src, fb_buf, gtc,
@@ -35,7 +35,7 @@
     zi_s, zi_r, t1_s, t1_r, t2_s, t2_r, t3_s, t3_r, t4_s, t4_r,
     iy_s, iy_r, iz_s, iz_r, tz_s, tz_r, ta_s, ta_r,
     quad_s, quad_r, row_s, row_r, col_s, col_r, tgt_s, tgt_r, g_s, g_r, gc_s, gc_r,
-    rs_s, rs_r, fb_s, fb_r, lb_s, lb_r, la_s, la_r,
+    rs_s, rs_r, fz_s, fz_r, fb_s, fb_r, lb_s, lb_r, la_s, la_r,
 ):
     b = lax.axis_index("batch")
     a = lax.axis_index("aug")
@@ -115,8 +115,12 @@
         copy(ref, ref, zi_s.at[m, 2, d], zi_r.at[m, 2, d], znext(1)).wait_recv()
 
     def img_start(m):
-        for d, h in ((0, 0), (1, 1), (0, 1), (1, 0)):
-            start(img_send(m, d, h))
+        start(img_send(m, 0, 0))
+        start(img_send(m, 1, 1))
+
+    def img_rest(m):
+        start(img_send(m, 0, 1))
+        start(img_send(m, 1, 0))
 
     def img_pass_on(m):
         img_recv(m, 0, 0)
@@ -275,13 +279,15 @@
     rowst[...] = jnp.ones_like(rowst)
     rowtmp[...] = jnp.zeros_like(rowtmp)
     img_start(1)
+    img_rest(1)
     text_start(1)
+    img_start(0)
     text_start(0)
     is_[z] = simg[...]
     it[z] = timg[...]
     text_spread(1)
     img_pass_on(1)
-    img_start(0)
+    img_rest(0)
     text_pass_on(1)
     text_spread(0)
     text_far(1)
@@ -292,6 +298,8 @@
     scores(1, zm1, ps, qs, student_scale)
     img_recv(1, 1, 0)
     scores(1, zp1, ps, qs, student_scale)
+    img_pass_on(0)
+    text_pass_on(0)
     img_recv_far(1, 0)
     img_recv_far(1, 1)
     scores(1, zp2, ps, qs, student_scale)
@@ -306,12 +314,11 @@
         isum[1, g] = total_img[HALF:, g * 128 : (g + 1) * 128]
     iy = copy(isum.at[1 - yh, z], isum_in.at[z], iy_s.at[0], iy_r.at[0], partner)
     start(iy)
-    text_pass_on(0)
-    stats_middle(1)
-    img_pass_on(0)
     text_far(0)
     text_wait(0)
+
     scores(0, z, pt, qt, teacher_scale)
+    stats_middle(1)
     img_recv(0, 0, 1)
     scores(0, zm1, pt, qt, teacher_scale)
     img_recv(0, 1, 0)
@@ -342,8 +349,6 @@
         + jnp.sum(jnp.sum(col_lse, axis=0, keepdims=True), axis=1, keepdims=True) * (1.0 / 16.0)
     )
 
-    stats_middle(0)
-
     for d in (2, 1, 3, 0):
         v = lax.rem(z + d, 4)
         factor = jnp.sum(jnp.where(lane == v, rowfac[1, :ROWS, :], 0.0), axis=1, keepdims=True)
@@ -363,6 +368,13 @@
     start(g_far(1))
     start(g_copy(0, 1))
     start(g_copy(1, 0))
+
+    stats_middle(0)
+
+    acc = dot(w[0], is_[0], TN)
+    for v in range(1, 4):
+        acc = acc + dot(w[v], is_[v], TN)
+    gtp[...] = acc
 
     stats_finish(0)
 
@@ -381,10 +393,6 @@
     for n in range(NCH):
         tgt[n] = own_targets(1 - yh, n)
         start(tgt_copy(n))
-    acc = dot(w[0], is_[0], TN)
-    for v in range(1, 4):
-        acc = acc + dot(w[v], is_[v], TN)
-    gtp[...] = acc
     for n in range(NCH):
         tgt_mine[n] = own_targets(yh, n)
 
@@ -421,8 +429,13 @@
         row = s * HALF
         for g in range(4):
             gtc[s % 2, s // 2, g] = res[row : row + HALF, g * 128 : (g + 1) * 128]
-    gc = copy(gtc.at[1 - k], gt_sib, gc_s.at[0], gc_r.at[0], sib)
-    start(gc)
+    def gc_copy(i):
+        rows = slice(i * 72, (i + 1) * 72)
+        return copy(gtc.at[1 - k, :, :, rows, :], gt_sib.at[:, :, rows, :], gc_s.at[i],
+                    gc_r.at[i], sib)
+
+    start(gc_copy(0))
+    start(gc_copy(1))
 
     target_loss = isum8[0] * tt_part[0]
     for g in range(1, 4):
@@ -437,10 +450,6 @@
 
     start_all(1, 16, lb_copy)
 
-    gc.wait_recv()
-    for blk in range(4):
-        for g in range(4):
-            gtc[k, blk, g] = gtc[k, blk, g] + gt_sib[blk, g]
     y = yh * 2 + yl
     pieces = gtc.at[k]
 
@@ -467,9 +476,14 @@
         return copy(rb_sum.at[lax.rem(x + d, 4)], rb2_in.at[d - 1],
                     rs_s.at[3, d - 1], rs_r.at[3, d - 1], xdev(d))
 
-    for d in (1, 3, 2):
-        start(ra_copy(d))
-        start(rb_copy(d))
+    for i in range(2):
+        gc_copy(i).wait_recv()
+        rows = slice(i * 72, (i + 1) * 72)
+        for blk in range(4):
+            for g in range(4):
+                gtc[k, blk, g, rows, :] = gtc[k, blk, g, rows, :] + gt_sib[blk, g, rows, :]
+        for d in ((1, 3, 2), (1, 3))[i]:
+            start((ra_copy, rb_copy)[i](d))
 
     total = tt_part[z]
     for d in (1, 3, 2):
@@ -480,6 +494,7 @@
     a_in = (1 - yh) * 4 + z
     ty = copy(tt_src, tt_all.at[a], ta_s.at[0], ta_r.at[a], partner)
     start(ty)
+    start(rb_copy(2))
 
     def ta_copy(d):
         return copy(tt_src, tt_all.at[a], ta_s.at[d], ta_r.at[a], znext(d))
@@ -528,39 +543,41 @@
     for d in (1, 3, 2):
         rb2_copy(d).wait_recv()
         last = last + rb2_in[d - 1]
-    fb_src[0:72, :] = first * student_scale
-    fb_src[72:144, :] = last * student_scale
-
-    def fb_to(i):
-        return (x * 4 + z, i)
-
-    def fb_copy(i):
-        return copy(fb_src, fb_buf.at[j * 2 + yh], fb_s.at[i], fb_r.at[j * 2 + yh], fb_to(i))
-
-    def is_self(i):
-        return (j == z) & (i == a)
-
-    def fb_go(i, _):
-        @pl.when(jnp.logical_not(is_self(i)))
-        def _():
-            fb_copy(i).start()
-
-        return 0
-
-    lax.fori_loop(0, 8, fb_go, 0)
-
-    def fb_gone(i, _):
-        @pl.when(jnp.logical_not(is_self(i)))
-        def _():
-            fb_copy(i).wait_send()
-
-        return 0
-
-    sent.append(lambda: lax.fori_loop(0, 8, fb_gone, 0))
-
-    @pl.when(j == z)
-    def _():
-        fb_buf[j * 2 + yh] = fb_src[...]
+    fb_src[z, 0:72, :] = first
+    fb_src[z, 72:144, :] = last
+
+    def fz_copy(d):
+        return copy(fb_src.at[z], fb_src.at[z], fz_s.at[d - 1], fz_r.at[d - 1], znext(d))
+
+    def fb_copy(c, h):
+        return copy(fb_src.at[c], fb_buf.at[j * 2 + yh], fb_s.at[c, h], fb_r.at[j * 2 + yh],
+                    dev(x, c, h, z))
+
+    def is_self(c, h):
+        return (j == c) & (yh == h)
+
+    def fb_send(c):
+        for h in range(2):
+            @pl.when(jnp.logical_not(is_self(c, h)))
+            def _():
+                fb_copy(c, h).start()
+
+    def fb_gone():
+        for c in range(4):
+            for h in range(2):
+                @pl.when(jnp.logical_not(is_self(c, h)))
+                def _():
+                    fb_copy(c, h).wait_send()
+
+    sent.append(fb_gone)
+    for d in (1, 3, 2):
+        start(fz_copy(d))
+    fb_send(z)
+    for d in (1, 3, 2):
+        c = lax.rem(z + 4 - d, 4)
+        copy(fb_src.at[c], fb_src.at[c], fz_s.at[d - 1], fz_r.at[d - 1], partner).wait_recv()
+        fb_send(c)
+    fb_buf[j * 2 + yh] = fb_src[j]
 
     acc = gsend[0]
     for i in range(2):
@@ -576,20 +593,19 @@
         rows = slice(h * HALF, (h + 1) * HALF)
         for g in range(4):
             lanes = slice(g * 128, (g + 1) * 128)
-            gi_out[rows, lanes] = (acc[rows, lanes] - tt_all[h * 4 + g]) * student_scale
+            grads_out[0, rows, lanes] = acc[rows, lanes] - tt_all[h * 4 + g]
 
     def la_wait(d, acc):
         la_copy(d).wait_recv()
         return acc + loss_a[d - 1]
 
-    loss_out[...] = lax.fori_loop(1, 8, la_wait, loss_src2[...]) * (1.0 / (2.0 * 8 * 4608))
+    whole = lax.fori_loop(1, 8, la_wait, loss_src2[...])
+    loss_out[0, 0] = jnp.sum(whole[0:1, 0:1]) * (1.0 / (2.0 * 8 * 4608))
 
     def fb_wait(s, _):
-        mine = (z == j) & (s == j * 2 + yh)
-
-        @pl.when(jnp.logical_not(mine))
+        @pl.when(s != j * 2 + yh)
         def _():
-            copy(fb_src, fb_buf.at[s], fb_s.at[s], fb_r.at[s], sib).wait_recv()
+            copy(fb_src.at[0], fb_buf.at[s], fb_s.at[0, 0], fb_r.at[s], partner).wait_recv()
 
         return 0
 
@@ -597,7 +613,7 @@
     for s in range(8):
         syl_, sk_, syh_ = s // 4, (s // 2) % 2, s % 2
         g = syh_ * 2 + syl_
-        gt_out[sk_ * HALF : (sk_ + 1) * HALF, g * 128 : (g + 1) * 128] = fb_buf[s]
+        grads_out[1, sk_ * HALF : (sk_ + 1) * HALF, g * 128 : (g + 1) * 128] = fb_buf[s]
 
     for gone in sent:
         gone()
@@ -608,16 +624,15 @@
     dma = pltpu.SemaphoreType.DMA
     V = pltpu.VMEM
     sw, twd = student_image.shape[2], teacher_image.shape[2]
-    loss, gi, gt = pl.pallas_call(
+    loss, grads = pl.pallas_call(
         kernel,
         name="distill",
         out_shape=(
-            jax.ShapeDtypeStruct((8, 128), F32),
-            jax.ShapeDtypeStruct((ROWS, sw), F32),
-            jax.ShapeDtypeStruct((ROWS, sw), F32),
+            jax.ShapeDtypeStruct((1, 1), F32),
+            jax.ShapeDtypeStruct((2, ROWS, sw), F32),
         ),
         in_specs=[vm] * 4,
-        out_specs=(vm, vm, vm),
+        out_specs=(pl.BlockSpec(memory_space=pltpu.SMEM), vm),
         scratch_shapes=[
             V((4, ROWS, twd), BF16), V((4, ROWS, sw), BF16),
             V((4 * ROWS, twd), BF16), V((4 * ROWS, sw), BF16),
@@ -634,7 +649,7 @@
             V((COLS, sw), F32), V((4, 4, HALF, 128), F32),
             V((3, 4, 72, 128), F32), V((3, 4, 72, 128), F32), V((4, 72, 128), F32),
             V((4, 72, 128), F32), V((3, 72, 128), F32), V((3, 72, 128), F32),
-            V((HALF, 128), F32), V((8, HALF, 128), F32),
+            V((4, HALF, 128), F32), V((8, HALF, 128), F32),
             V((2, 4, 4, HALF, 128), F32),
             V((384, 128), F32), V((2, 8, 384), F32), V((2, 3, 8, 384), F32),
             V((2, 384, 128), F32), V((128, 384), F32),
@@ -646,8 +661,8 @@
             dma((2, 2)), dma((2, 2)),
             dma((1,)), dma((1,)), dma((3,)), dma((3,)), dma((3,)), dma((3,)), dma((7,)), dma((8,)),
             dma((2, 3)), dma((2, 3)), dma((2, 3)), dma((2, 3)), dma((2, 3)), dma((2, 3)),
-            dma((3,)), dma((3,)), dma((3, 2)), dma((3, 2)), dma((1,)), dma((1,)),
-            dma((4, 3)), dma((4, 3)), dma((8,)), dma((8,)),
+            dma((3,)), dma((3,)), dma((3, 2)), dma((3, 2)), dma((2,)), dma((2,)),
+            dma((4, 3)), dma((4, 3)), dma((3,)), dma((3,)), dma((4, 2)), dma((8,)),
             dma((15,)), dma((15,)), dma((7,)), dma((7,)),
         ],
         compiler_params=pltpu.CompilerParams(
@@ -657,7 +672,8 @@
             flops=8 * 10**9, bytes_accessed=4 * 2**20, transcendentals=6 * 10**6
         ),
     )(student_image[0], student_text, teacher_image[0], teacher_text)
-    return loss[0, 0], gi[None], gt
+    scale = 3.0 / math.sqrt(sw)
+    return loss.reshape(()), (grads[0] * scale)[None], grads[1] * scale
 
 
 def solution(mesh):

time: 115 us -> 109 us (0.948); the launches traced: 113 us -> 109 us
  Pallas kernels: 108 us -> 104 us
  local copies, waits for them, and re-layouts: 3.98 us -> 0 us
  other arithmetic: 0 us -> 2.38 us
  between operations: 0.64 us -> 2.37 us
    pallas_call x1, Pallas kernels: 108 us -> 104 us  [per_device(): pl.pallas_call(kernel, name='distill', out_shape=(jax.ShapeDtypeStruct((1...]
    unnamed x4 -> x0, local copies, waits for them, and re-layouts: 2.8 us -> none
    mul x0 -> x1, other arithmetic: none -> 2.38 us  [per_device(): return (loss.reshape(()), (grads[0] * scale)[None], grads[1] * scale)]
    slice x1 -> x0, local copies, waits for them, and re-layouts: 1.18 us -> none  [per_device(): return (loss[0, 0], gi[None], gt)]
where the time goes in v4:
time: 109 us
  Pallas kernels  104 us (95%)
  other arithmetic  2.38 us (2%)
  between operations  2.37 us (2%)
    pallas_call x1, Pallas kernels, per_device(): pl.pallas_call(kernel, name='distill', out_shape=(jax.ShapeDtypeStruct((1...  104 us
    mul x1, other arithmetic, per_device(): return (loss.reshape(()), (grads[0] * scale)[None], grads[1] * scale)  2.38 us

profile of v4, /device:TPU:97, one launch (start us, length us, event | category | flops | bytes accessed | tf_op | source)
XLA Modules:
  0.0 109.2 jit_solution(11704202446916560936)
XLA Ops:
  0.6 104.4 %distill.1 = (f32[1,1]{1,0:T(1,128)}, f32[2,288,512]{2,1,0:T(8,128)}) custom-call(bf16[288,512]{1,0:T(8,128)(2,1)} %bitcast.6, bf16[288,512]{1,0:T(8,128)(2,1)} %stext.1, bf16[288,1280]{1,0:T(8,128)(2,1)} %bitcast.5, bf16[288,1280]{1,0:T(8,128)(2,1)} %ttext.1), custom_call_target="tpu_custom_call" | custom-call | flops 8000000000 | bytes 4194304 | tf_op jit(solution)/shard_map/distill/pallas_call | solution.py:627
  105.1 2.4 %multiply_bitcast_fusion = (f32[288,512]{1,0:T(8,128)}, f32[1,288,512]{2,1,0:T(8,128)}) fusion(f32[2,288,512]{2,1,0:T(8,128)} %get-tuple-element.6), kind=kLoop, calls=%fused_computation | loop fusion | flops 294912 | bytes 2359296 | tf_op jit(solution)/shard_map/mul | solution.py:676

commit v5 on v4

--- a/solution.py
+++ b/solution.py
@@ -30,11 +30,11 @@
     it, is_, tt, ts, pt, qt, ps, qs, w, tgt, tgt_mine, tgt_in, tw,
     isum, isum_in, isum8, hi, lo, tt_part, tt_in, tt_src, tt_all,
     gsend, grecv, gfar_in, gtp, gt_sib, ra_in, rb_in, ra_sum, rb_sum, ra2_in, rb2_in, fb_src, fb_buf, gtc,
-    rowst, rowsend, rowrecv, rowfac, rowtmp, colst, quad_in, colq, colx_in, colfac,
+    rowst, rowsend, rowrecv, rowfac, rowtmp, colst, quad_in, colq, colx_in, colfac, cfar, cfar_in,
     loss_src, loss_b, loss_src2, loss_a,
-    zi_s, zi_r, t1_s, t1_r, t2_s, t2_r, t3_s, t3_r, t4_s, t4_r,
+    zi_s, zi_r, t1_s, t1_r, t2_s, t2_r, t3_s, t3_r, t4_s, t4_r, t5_s, t5_r,
     iy_s, iy_r, iz_s, iz_r, tz_s, tz_r, ta_s, ta_r,
-    quad_s, quad_r, row_s, row_r, col_s, col_r, tgt_s, tgt_r, g_s, g_r, gc_s, gc_r,
+    far_s, far_r, quad_s, quad_r, row_s, row_r, col_s, col_r, tgt_s, tgt_r, g_s, g_r, gc_s, gc_r,
     rs_s, rs_r, fz_s, fz_r, fb_s, fb_r, lb_s, lb_r, la_s, la_r,
 ):
     b = lax.axis_index("batch")
@@ -63,6 +63,18 @@
         c.start()
         sent.append(c.wait_send)
 
+    def start_if(cond, c):
+        @pl.when(cond)
+        def _():
+            c.start()
+
+        def gone():
+            @pl.when(cond)
+            def _():
+                c.wait_send()
+
+        sent.append(gone)
+
     def start_all(lo, hi, make):
         def go(i, _):
             make(i).start()
@@ -179,25 +191,57 @@
         blk = lax.rem(x + 4 - d, 4)
         return copy(tslab(m, blk, k), tslab(m, blk, k), t3_s.at[m, d], t3_r.at[m, d], sib)
 
-    def text_spread(m):
-        @pl.when(jnp.logical_not(is_source))
+    holds = yl == syl
+    lacks = yl != syl
+
+    def text_cross(d):
+        slab = tslab(1, lax.rem(x + 4 - d, 4), k)
+        to = dev(x, (1 - syl) * 2 + k, yh + k * (1 - 2 * yh), z)
+        return copy(slab, slab, t5_s.at[d - 1], t5_r.at[d - 1], to)
+
+    def crossed(d):
+        @pl.when(lacks)
+        def _():
+            slab = tslab(1, lax.rem(x + 4 - d, 4), k)
+            copy(slab, slab, t5_s.at[d - 1], t5_r.at[d - 1], sib).wait_recv()
+
+    def text_spread(m, here):
+        @pl.when(here & jnp.logical_not(is_source))
         def _():
             copy(tslab(m, x, k), tslab(m, x, k), t1_s.at[m, 0], t1_r.at[m], sib).wait_recv()
 
         for d in (1, 3):
-            start(text_x(m, d))
-        start(text_sib(m, 0))
+            if m == 0 or here is holds:
+                start_if(here, text_x(m, d))
+        start_if(here, text_sib(m, 0))
 
     def text_pass_on(m):
         for d in (1, 3):
-            text_got(m, d)
-            start(text_relay(m, d // 2))
+            if m:
+                @pl.when(holds)
+                def _():
+                    text_got(m, d)
+
+                start_if(holds, text_relay(m, d // 2))
+                start_if(holds, text_cross(d))
+                crossed(d)
+            else:
+                text_got(m, d)
+                start(text_relay(m, d // 2))
             start(text_sib(m, d))
 
     def text_far(m):
-        for i in range(2):
-            ref = tlanes(m, lax.rem(x + 2, 4), i)
-            copy(ref, ref, t4_s.at[m, i], t4_r.at[m, i], sib).wait_recv()
+        def arrived():
+            for i in range(2):
+                ref = tlanes(m, lax.rem(x + 2, 4), i)
+                copy(ref, ref, t4_s.at[m, i], t4_r.at[m, i], sib).wait_recv()
+
+        if m:
+            pl.when(holds)(arrived)
+            start_if(holds, text_cross(2))
+            crossed(2)
+        else:
+            arrived()
         start(text_sib(m, 2))
 
     def text_wait(m):
@@ -211,7 +255,7 @@
     def fold(op, t):
         return functools.reduce(op, [t[:, i * 128 : (i + 1) * 128] for i in range(COLS // 128)])
 
-    def scores(m, v, pr, qr, scale):
+    def scores(m, v, pr, qr, scale, far=False):
         t = dot(imgs[m][v], texts[m][...], NT) * scale
         cm = jnp.max(t, axis=0, keepdims=True)
         top = jnp.max(fold(jnp.maximum, t), axis=1, keepdims=True)
@@ -219,8 +263,13 @@
         qr[v] = q
         p = jnp.exp(t - top)
         pr[v] = p
-        colst[m, pl.ds(v, 1), :] = cm
-        colst[m, pl.ds(v + 4, 1), :] = jnp.sum(q, axis=0, keepdims=True)
+        cs = jnp.sum(q, axis=0, keepdims=True)
+        if far:
+            cfar[0:1, :] = cm
+            cfar[1:2, :] = cs
+        else:
+            colst[m, pl.ds(v, 1), :] = cm
+            colst[m, pl.ds(v + 4, 1), :] = cs
         total = jnp.sum(fold(jnp.add, p), axis=1, keepdims=True)
         rowst[:ROWS, :] = jnp.where(
             lane == v, top, jnp.where(lane == v + 4, total, rowst[:ROWS, :])
@@ -245,9 +294,29 @@
             total = total + t[4:] * jnp.exp(t[:4] - top)
         return top, total
 
-    def stats_start(m):
+    def far_copy(d):
+        return copy(cfar, cfar_in.at[d - 1], far_s.at[d - 1], far_r.at[d - 1],
+                    (lax.rem(b + d, 16), a))
+
+    def far_finish():
+        def arrived(d, top):
+            far_copy(d).wait_recv()
+            return jnp.maximum(top, cfar_in[d - 1, 0:1, :])
+
+        mine = cfar[0:1, :]
+        top = lax.fori_loop(1, 16, arrived, mine)
+
+        def add(d, total):
+            return total + cfar_in[d, 1:2, :] * jnp.exp(cfar_in[d, 0:1, :] - top)
+
+        total = lax.fori_loop(0, 15, add, cfar[1:2, :] * jnp.exp(mine - top))
+        colfac[0, pl.ds(zp2, 1), :] = jnp.exp(mine - top - jnp.log(total))
+
+    def cols_start(m):
         for d in (1, 2, 3):
             start(quad_copy(m, d))
+
+    def rows_start(m):
         rowsend[m] = jnp.transpose(rowst[...])[:8]
         for d in (1, 3, 2):
             start(row_copy(m, d))
@@ -278,6 +347,7 @@
 
     rowst[...] = jnp.ones_like(rowst)
     rowtmp[...] = jnp.zeros_like(rowtmp)
+    colst[0] = jnp.ones_like(colst[0])
     img_start(1)
     img_rest(1)
     text_start(1)
@@ -285,11 +355,13 @@
     text_start(0)
     is_[z] = simg[...]
     it[z] = timg[...]
-    text_spread(1)
+    text_spread(1, holds)
+    text_spread(1, lacks)
+    text_spread(0, lacks)
     img_pass_on(1)
     img_rest(0)
     text_pass_on(1)
-    text_spread(0)
+    text_spread(0, holds)
     text_far(1)
     text_wait(1)
 
@@ -303,7 +375,8 @@
     img_recv_far(1, 0)
     img_recv_far(1, 1)
     scores(1, zp2, ps, qs, student_scale)
-    stats_start(1)
+    cols_start(1)
+    rows_start(1)
 
     partner = (b, (1 - yh) * 4 + z)
     total_img = (
@@ -323,10 +396,13 @@
     scores(0, zm1, pt, qt, teacher_scale)
     img_recv(0, 1, 0)
     scores(0, zp1, pt, qt, teacher_scale)
+    cols_start(0)
+    stats_middle(0)
     img_recv_far(0, 0)
     img_recv_far(0, 1)
-    scores(0, zp2, pt, qt, teacher_scale)
-    stats_start(0)
+    scores(0, zp2, pt, qt, teacher_scale, far=True)
+    start_all(1, 16, far_copy)
+    rows_start(0)
 
     def iz_copy(d):
         slot = isum_in.at[z]
@@ -369,14 +445,9 @@
     start(g_copy(0, 1))
     start(g_copy(1, 0))
 
-    stats_middle(0)
-
-    acc = dot(w[0], is_[0], TN)
-    for v in range(1, 4):
-        acc = acc + dot(w[v], is_[v], TN)
-    gtp[...] = acc
 
     stats_finish(0)
+    far_finish()
 
 
     def tgt_copy(n):
@@ -393,6 +464,10 @@
     for n in range(NCH):
         tgt[n] = own_targets(1 - yh, n)
         start(tgt_copy(n))
+    acc = dot(w[0], is_[0], TN)
+    for v in range(1, 4):
+        acc = acc + dot(w[v], is_[v], TN)
+    gtp[...] = acc
     for n in range(NCH):
         tgt_mine[n] = own_targets(yh, n)
 
@@ -655,11 +730,13 @@
             V((2, 384, 128), F32), V((128, 384), F32),
             V((2, 8, COLS), F32), V((2, 3, 8, COLS), F32), V((2, 8, COLS), F32),
             V((2, 3, 8, COLS), F32), V((2, 8, COLS), F32),
+            V((2, COLS), F32), V((15, 2, COLS), F32),
             V((8, 128), F32), V((15, 8, 128), F32), V((8, 128), F32), V((7, 8, 128), F32),
             dma((2, 3, 2)), dma((2, 3, 2)),
             dma((2, 3)), dma((2,)), dma((2, 3)), dma((2, 3)), dma((2, 4)), dma((2, 4)),
-            dma((2, 2)), dma((2, 2)),
+            dma((2, 2)), dma((2, 2)), dma((3,)), dma((3,)),
             dma((1,)), dma((1,)), dma((3,)), dma((3,)), dma((3,)), dma((3,)), dma((7,)), dma((8,)),
+            dma((15,)), dma((15,)),
             dma((2, 3)), dma((2, 3)), dma((2, 3)), dma((2, 3)), dma((2, 3)), dma((2, 3)),
             dma((3,)), dma((3,)), dma((3, 2)), dma((3, 2)), dma((2,)), dma((2,)),
             dma((4, 3)), dma((4, 3)), dma((3,)), dma((3,)), dma((4, 2)), dma((8,)),

time: 109 us -> 106 us (0.972)
  Pallas kernels: 104 us -> 102 us
    pallas_call x1, Pallas kernels: 104 us -> 102 us  [per_device(): pl.pallas_call(kernel, name='distill', out_shape=(jax.ShapeDtypeStruct((1...]
where the time goes in v5:
time: 106 us
  Pallas kernels  102 us (96%)
  other arithmetic  2.38 us (2%)
  between operations  2.37 us (2%)
    pallas_call x1, Pallas kernels, per_device(): pl.pallas_call(kernel, name='distill', out_shape=(jax.ShapeDtypeStruct((1...  102 us
    mul x1, other arithmetic, per_device(): return (loss.reshape(()), (grads[0] * scale)[None], grads[1] * scale)  2.38 us

profile of v5, /device:TPU:97, one launch (start us, length us, event | category | flops | bytes accessed | tf_op | source)
XLA Modules:
  0.0 106.3 jit_solution(18181112279613199614)
XLA Ops:
  0.6 101.6 %distill.1 = (f32[1,1]{1,0:T(1,128)}, f32[2,288,512]{2,1,0:T(8,128)}) custom-call(bf16[288,512]{1,0:T(8,128)(2,1)} %bitcast.6, bf16[288,512]{1,0:T(8,128)(2,1)} %stext.1, bf16[288,1280]{1,0:T(8,128)(2,1)} %bitcast.5, bf16[288,1280]{1,0:T(8,128)(2,1)} %ttext.1), custom_call_target="tpu_custom_call" | custom-call | flops 8000000000 | bytes 4194304 | tf_op jit(solution)/shard_map/distill/pallas_call | solution.py:702
  102.2 2.4 %multiply_bitcast_fusion = (f32[288,512]{1,0:T(8,128)}, f32[1,288,512]{2,1,0:T(8,128)}) fusion(f32[2,288,512]{2,1,0:T(8,128)} %get-tuple-element.6), kind=kLoop, calls=%fused_computation | loop fusion | flops 294912 | bytes 2359296 | tf_op jit(solution)/shard_map/mul | solution.py:753

commit v6 on v5

--- a/solution.py
+++ b/solution.py
@@ -32,7 +32,7 @@
     gsend, grecv, gfar_in, gtp, gt_sib, ra_in, rb_in, ra_sum, rb_sum, ra2_in, rb2_in, fb_src, fb_buf, gtc,
     rowst, rowsend, rowrecv, rowfac, rowtmp, colst, quad_in, colq, colx_in, colfac, cfar, cfar_in,
     loss_src, loss_b, loss_src2, loss_a,
-    zi_s, zi_r, t1_s, t1_r, t2_s, t2_r, t3_s, t3_r, t4_s, t4_r, t5_s, t5_r,
+    own_s, zi_s, zi_r, t1_s, t1_r, t2_s, t2_r, t3_s, t3_r, t4_s, t4_r, t5_s, t5_r,
     iy_s, iy_r, iz_s, iz_r, tz_s, tz_r, ta_s, ta_r,
     far_s, far_r, quad_s, quad_r, row_s, row_r, col_s, col_r, tgt_s, tgt_r, g_s, g_r, gc_s, gc_r,
     rs_s, rs_r, fz_s, fz_r, fb_s, fb_r, lb_s, lb_r, la_s, la_r,
@@ -156,12 +156,20 @@
                  t1_s.at[m, 2], t1_r.at[m], dev(x, (1 - syl) * 2 + 1, 1 - yh, z)),
         )
 
+    def text_own(m):
+        return pltpu.make_async_copy(
+            own_text[m].at[pl.ds(k * HALF, HALF)], tslab(m, x, k), own_s.at[2 + m]
+        )
+
+    def img_own(m):
+        return pltpu.make_async_copy(own[m], imgs[m].at[z], own_s.at[m])
+
     def text_start(m):
         @pl.when(is_source)
         def _():
             for c in text_first(m):
                 c.start()
-            tslab(m, x, k)[...] = own_text[m][pl.ds(k * HALF, HALF)]
+            text_own(m).start()
 
         def gone():
             @pl.when(is_source)
@@ -209,6 +217,10 @@
         @pl.when(here & jnp.logical_not(is_source))
         def _():
             copy(tslab(m, x, k), tslab(m, x, k), t1_s.at[m, 0], t1_r.at[m], sib).wait_recv()
+
+        @pl.when(here & is_source)
+        def _():
+            text_own(m).wait()
 
         for d in (1, 3):
             if m == 0 or here is holds:
@@ -353,8 +365,8 @@
     text_start(1)
     img_start(0)
     text_start(0)
-    is_[z] = simg[...]
-    it[z] = timg[...]
+    img_own(1).start()
+    img_own(0).start()
     text_spread(1, holds)
     text_spread(1, lacks)
     text_spread(0, lacks)
@@ -365,6 +377,7 @@
     text_far(1)
     text_wait(1)
 
+    img_own(1).wait()
     scores(1, z, ps, qs, student_scale)
     img_recv(1, 0, 1)
     scores(1, zm1, ps, qs, student_scale)
@@ -390,6 +403,7 @@
     text_far(0)
     text_wait(0)
 
+    img_own(0).wait()
     scores(0, z, pt, qt, teacher_scale)
     stats_middle(1)
     img_recv(0, 0, 1)
@@ -704,9 +718,9 @@
         name="distill",
         out_shape=(
             jax.ShapeDtypeStruct((1, 1), F32),
-            jax.ShapeDtypeStruct((2, ROWS, sw), F32),
+            pltpu.VMEM((2, ROWS, sw), F32),
         ),
-        in_specs=[vm] * 4,
+        in_specs=[pl.BlockSpec(memory_space=pl.ANY)] * 4,
         out_specs=(pl.BlockSpec(memory_space=pltpu.SMEM), vm),
         scratch_shapes=[
             V((4, ROWS, twd), BF16), V((4, ROWS, sw), BF16),
@@ -732,7 +746,7 @@
             V((2, 3, 8, COLS), F32), V((2, 8, COLS), F32),
             V((2, COLS), F32), V((15, 2, COLS), F32),
             V((8, 128), F32), V((15, 8, 128), F32), V((8, 128), F32), V((7, 8, 128), F32),
-            dma((2, 3, 2)), dma((2, 3, 2)),
+            dma((4,)), dma((2, 3, 2)), dma((2, 3, 2)),
             dma((2, 3)), dma((2,)), dma((2, 3)), dma((2, 3)), dma((2, 4)), dma((2, 4)),
             dma((2, 2)), dma((2, 2)), dma((3,)), dma((3,)),
             dma((1,)), dma((1,)), dma((3,)), dma((3,)), dma((3,)), dma((3,)), dma((7,)), dma((8,)),
@@ -743,7 +757,7 @@
             dma((15,)), dma((15,)), dma((7,)), dma((7,)),
         ],
         compiler_params=pltpu.CompilerParams(
-            collective_id=0, has_side_effects=True, vmem_limit_bytes=60 * 1024 * 1024
+            collective_id=0, has_side_effects=True, vmem_limit_bytes=58 * 1024 * 1024
         ),
         cost_estimate=pl.CostEstimate(
             flops=8 * 10**9, bytes_accessed=4 * 2**20, transcendentals=6 * 10**6

time: 106 us -> 103 us (0.972)
  Pallas kernels: 102 us -> 98.9 us
  other arithmetic: 2.38 us -> 1.14 us
    pallas_call x1, Pallas kernels: 102 us -> 98.9 us  [per_device(): pl.pallas_call(kernel, name='distill', out_shape=(jax.ShapeDtypeStruct((1...]
    mul x1, other arithmetic: 2.38 us -> 1.14 us  [per_device(): return (loss.reshape(()), (grads[0] * scale)[None], grads[1] * scale)]
where the time goes in v6:
time: 103 us; the launch traced here: 102 us
  Pallas kernels  98.9 us (96%)
  between operations  2.4 us (2%)
  other arithmetic  1.14 us (1%)
    pallas_call x1, Pallas kernels, per_device(): pl.pallas_call(kernel, name='distill', out_shape=(jax.ShapeDtypeStruct((1...  98.9 us

profile of v6, /device:TPU:97, one launch (start us, length us, event | category | flops | bytes accessed | tf_op | source)
XLA Modules:
  0.0 102.4 jit_solution(11070104384989150423)
XLA Ops:
  0.6 98.9 %distill.1 = (f32[1,1]{1,0:T(1,128)}, f32[2,288,512]{2,1,0:T(8,128)S(1)}) custom-call(bf16[288,512]{1,0:T(8,128)(2,1)} %bitcast.6, bf16[288,512]{1,0:T(8,128)(2,1)} %stext.1, bf16[288,1280]{1,0:T(8,128)(2,1)} %bitcast.5, bf16[288,1280]{1,0:T(8,128)(2,1)} %ttext.1), custom_call_target="tpu_custom_call" | custom-call | flops 8000000000 | bytes 4194304 | tf_op jit(solution)/shard_map/distill/pallas_call | solution.py:716
  99.5 1.1 %multiply_bitcast_fusion = (f32[288,512]{1,0:T(8,128)}, f32[1,288,512]{2,1,0:T(8,128)}) fusion(f32[2,288,512]{2,1,0:T(8,128)S(1)} %get-tuple-element.6), kind=kLoop, calls=%fused_computation | loop fusion | flops 294912 | bytes 2359296 | tf_op jit(solution)/shard_map/mul | solution.py:767

commit v7 on v6

--- a/solution.py
+++ b/solution.py
@@ -75,17 +75,21 @@
 
         sent.append(gone)
 
-    def start_all(lo, hi, make):
+    def start_group(copies, into, ss, rs):
+        for c in copies:
+            c.start()
+        sent.append(copy(into, into, ss, rs, sib).wait_send)
+
+    def take_group(into, ss, rs):
+        copy(into, into, ss, rs, sib).wait_recv()
+
+    def start_all(lo, hi, make, into, ss, rs):
         def go(i, _):
             make(i).start()
             return 0
 
-        def gone(i, _):
-            make(i).wait_send()
-            return 0
-
         lax.fori_loop(lo, hi, go, 0)
-        sent.append(lambda: lax.fori_loop(lo, hi, gone, 0))
+        sent.append(copy(into, into, ss, rs, sib).wait_send)
 
     barrier = pltpu.get_barrier_semaphore()
 
@@ -288,15 +292,15 @@
         )
 
     def row_copy(m, d):
-        return copy(rowsend.at[m], rowrecv.at[m, d - 1], row_s.at[m, d - 1], row_r.at[m, d - 1],
+        return copy(rowsend.at[m], rowrecv.at[m, d - 1], row_s.at[m], row_r.at[m],
                     znext(d))
 
     def quad_copy(m, d):
-        return copy(colst.at[m], quad_in.at[m, d - 1], quad_s.at[m, d - 1], quad_r.at[m, d - 1],
+        return copy(colst.at[m], quad_in.at[m, d - 1], quad_s.at[m], quad_r.at[m],
                     (x * 4 + lax.rem(j + d, 4), a))
 
     def col_copy(m, d):
-        return copy(colq.at[m], colx_in.at[m, d - 1], col_s.at[m, d - 1], col_r.at[m, d - 1],
+        return copy(colq.at[m], colx_in.at[m, d - 1], col_s.at[m], col_r.at[m],
                     (lax.rem(x + d, 4) * 4 + j, a))
 
     def merged(mine, others):
@@ -307,12 +311,13 @@
         return top, total
 
     def far_copy(d):
-        return copy(cfar, cfar_in.at[d - 1], far_s.at[d - 1], far_r.at[d - 1],
+        return copy(cfar, cfar_in.at[d - 1], far_s.at[0], far_r.at[0],
                     (lax.rem(b + d, 16), a))
 
     def far_finish():
+        take_group(cfar_in, far_s.at[0], far_r.at[0])
+
         def arrived(d, top):
-            far_copy(d).wait_recv()
             return jnp.maximum(top, cfar_in[d - 1, 0:1, :])
 
         mine = cfar[0:1, :]
@@ -325,33 +330,27 @@
         colfac[0, pl.ds(zp2, 1), :] = jnp.exp(mine - top - jnp.log(total))
 
     def cols_start(m):
-        for d in (1, 2, 3):
-            start(quad_copy(m, d))
+        start_group([quad_copy(m, d) for d in (1, 2, 3)], quad_in.at[m], quad_s.at[m], quad_r.at[m])
 
     def rows_start(m):
         rowsend[m] = jnp.transpose(rowst[...])[:8]
-        for d in (1, 3, 2):
-            start(row_copy(m, d))
+        start_group([row_copy(m, d) for d in (1, 3, 2)], rowrecv.at[m], row_s.at[m], row_r.at[m])
 
     def stats_middle(m):
-        for d in (1, 2, 3):
-            quad_copy(m, d).wait_recv()
+        take_group(quad_in.at[m], quad_s.at[m], quad_r.at[m])
         top, total = merged(colst[m], [quad_in[m, d] for d in range(3)])
         colq[m, 0:4, :] = top
         colq[m, 4:8, :] = total
-        for d in (1, 3, 2):
-            start(col_copy(m, d))
+        start_group([col_copy(m, d) for d in (1, 3, 2)], colx_in.at[m], col_s.at[m], col_r.at[m])
 
     def stats_finish(m):
-        for d in (1, 3, 2):
-            row_copy(m, d).wait_recv()
+        take_group(rowrecv.at[m], row_s.at[m], row_r.at[m])
         mine = rowsend[m]
         top, total = merged(mine, [rowrecv[m, d] for d in range(3)])
         row_lse = top + jnp.log(total)
         rowtmp[0:4, :] = jnp.exp(mine[:4] - row_lse)
         rowfac[m] = jnp.transpose(rowtmp[...])
-        for d in (1, 3, 2):
-            col_copy(m, d).wait_recv()
+        take_group(colx_in.at[m], col_s.at[m], col_r.at[m])
         top, total = merged(colq[m], [colx_in[m, d] for d in range(3)])
         col_lse = top + jnp.log(total)
         colfac[m, 0:4, :] = jnp.exp(colst[m, 0:4, :] - col_lse)
@@ -415,7 +414,7 @@
     img_recv_far(0, 0)
     img_recv_far(0, 1)
     scores(0, zp2, pt, qt, teacher_scale, far=True)
-    start_all(1, 16, far_copy)
+    start_all(1, 16, far_copy, cfar_in, far_s.at[0], far_r.at[0])
     rows_start(0)
 
     def iz_copy(d):
@@ -502,17 +501,6 @@
     for n in range(NCH):
         tgt_copy(n).wait_recv()
         tw[n * 48 : (n + 1) * 48] = ((tgt_mine[n] + tgt_in[n]) * 0.125).astype(BF16)
-    target_text = dot(tw[...], ts[...], NN)
-    for g in range(4):
-        tt_part[g] = target_text[:, g * 128 : (g + 1) * 128]
-
-    def tz_copy(d):
-        return copy(tt_part.at[lax.rem(z + d, 4)], tt_in.at[d - 1], tz_s.at[d - 1],
-                    tz_r.at[d - 1], znext(d))
-
-    for d in (2, 1, 3):
-        start(tz_copy(d))
-
     res = gtp[...] - dot(tw[...], hi[...], TN) - dot(tw[...], lo[...], TN)
     for s in range(8):
         row = s * HALF
@@ -526,6 +514,16 @@
     start(gc_copy(0))
     start(gc_copy(1))
 
+    target_text = dot(tw[...], ts[...], NN)
+    for g in range(4):
+        tt_part[g] = target_text[:, g * 128 : (g + 1) * 128]
+
+    def tz_copy(d):
+        return copy(tt_part.at[lax.rem(z + d, 4)], tt_in.at[d - 1], tz_s.at[0],
+                    tz_r.at[0], znext(d))
+
+    start_group([tz_copy(d) for d in (2, 1, 3)], tt_in, tz_s.at[0], tz_r.at[0])
+
     target_loss = isum8[0] * tt_part[0]
     for g in range(1, 4):
         target_loss = target_loss + isum8[g] * tt_part[g]
@@ -534,10 +532,10 @@
     loss_src[...] = jnp.broadcast_to(part, (8, 128))
 
     def lb_copy(d):
-        return copy(loss_src, loss_b.at[d - 1], lb_s.at[d - 1], lb_r.at[d - 1],
+        return copy(loss_src, loss_b.at[d - 1], lb_s.at[0], lb_r.at[0],
                     (lax.rem(b + d, 16), a))
 
-    start_all(1, 16, lb_copy)
+    start_all(1, 16, lb_copy, loss_b, lb_s.at[0], lb_r.at[0])
 
     y = yh * 2 + yl
     pieces = gtc.at[k]
@@ -551,19 +549,19 @@
 
     def ra_copy(d):
         return copy(pieces.at[lax.rem(x + d, 4), :, 0:72, :], ra_in.at[d - 1],
-                    rs_s.at[0, d - 1], rs_r.at[0, d - 1], xdev(d))
+                    rs_s.at[0], rs_r.at[0], xdev(d))
 
     def rb_copy(d):
         return copy(pieces.at[:, lax.rem(y + d, 4), 72:144, :], rb_in.at[d - 1],
-                    rs_s.at[1, d - 1], rs_r.at[1, d - 1], ydev(d))
+                    rs_s.at[1], rs_r.at[1], ydev(d))
 
     def ra2_copy(d):
         return copy(ra_sum.at[lax.rem(y + d, 4)], ra2_in.at[d - 1],
-                    rs_s.at[2, d - 1], rs_r.at[2, d - 1], ydev(d))
+                    rs_s.at[2], rs_r.at[2], ydev(d))
 
     def rb2_copy(d):
         return copy(rb_sum.at[lax.rem(x + d, 4)], rb2_in.at[d - 1],
-                    rs_s.at[3, d - 1], rs_r.at[3, d - 1], xdev(d))
+                    rs_s.at[3], rs_r.at[3], xdev(d))
 
     for i in range(2):
         gc_copy(i).wait_recv()
@@ -571,19 +569,21 @@
         for blk in range(4):
             for g in range(4):
                 gtc[k, blk, g, rows, :] = gtc[k, blk, g, rows, :] + gt_sib[blk, g, rows, :]
-        for d in ((1, 3, 2), (1, 3))[i]:
-            start((ra_copy, rb_copy)[i](d))
+        if i == 0:
+            start_group([ra_copy(d) for d in (1, 3, 2)], ra_in, rs_s.at[0], rs_r.at[0])
+        else:
+            start_group([rb_copy(d) for d in (1, 3)], rb_in, rs_s.at[1], rs_r.at[1])
 
     total = tt_part[z]
-    for d in (1, 3, 2):
-        tz_copy(d).wait_recv()
+    take_group(tt_in, tz_s.at[0], tz_r.at[0])
+    for d in (1, 3, 2):
         total = total + tt_in[d - 1]
     tt_src[...] = total
 
     a_in = (1 - yh) * 4 + z
     ty = copy(tt_src, tt_all.at[a], ta_s.at[0], ta_r.at[a], partner)
     start(ty)
-    start(rb_copy(2))
+    rb_copy(2).start()
 
     def ta_copy(d):
         return copy(tt_src, tt_all.at[a], ta_s.at[d], ta_r.at[a], znext(d))
@@ -598,45 +598,50 @@
         start(ta_copy(d))
     tt_all[a] = total
 
+    take_group(loss_b, lb_s.at[0], lb_r.at[0])
+
     def lb_wait(d, acc):
-        lb_copy(d).wait_recv()
         return acc + loss_b[d - 1]
 
     loss_src2[...] = lax.fori_loop(1, 16, lb_wait, loss_src[...])
 
     def la_copy(d):
-        return copy(loss_src2, loss_a.at[d - 1], la_s.at[d - 1], la_r.at[d - 1],
+        return copy(loss_src2, loss_a.at[d - 1], la_s.at[0], la_r.at[0],
                     (b, lax.rem(a + d, 8)))
 
-    start_all(1, 8, la_copy)
+    start_all(1, 8, la_copy, loss_a, la_s.at[0], la_r.at[0])
 
     ra_sum[...] = gtc[k, x, :, 0:72, :]
     rb_sum[...] = gtc[k, :, y, 72:144, :]
-    for d in (1, 3, 2):
-        ra_copy(d).wait_recv()
+    take_group(ra_in, rs_s.at[0], rs_r.at[0])
+    for d in (1, 3, 2):
         ra_sum[...] = ra_sum[...] + ra_in[d - 1]
-    for d in (1, 3, 2):
-        start(ra2_copy(d))
-    for d in (1, 3, 2):
-        rb_copy(d).wait_recv()
+    start_group([ra2_copy(d) for d in (1, 3, 2)], ra2_in, rs_s.at[2], rs_r.at[2])
+    take_group(rb_in, rs_s.at[1], rs_r.at[1])
+    for d in (1, 3, 2):
         rb_sum[...] = rb_sum[...] + rb_in[d - 1]
-    for d in (1, 3, 2):
-        start(rb2_copy(d))
+    start_group([rb2_copy(d) for d in (1, 3, 2)], rb2_in, rs_s.at[3], rs_r.at[3])
     t_wait(a_in)
     for d in (1, 3, 2):
         start(tb_copy(d))
-    first, last = ra_sum[y], rb_sum[x]
-    for d in (1, 3, 2):
-        ra2_copy(d).wait_recv()
+    def fz_copy(c, i, d):
+        ref = fb_src.at[c, i * 72 : (i + 1) * 72]
+        return copy(ref, ref, fz_s.at[i, d - 1], fz_r.at[i, d - 1], znext(d))
+
+    first = ra_sum[y]
+    take_group(ra2_in, rs_s.at[2], rs_r.at[2])
+    for d in (1, 3, 2):
         first = first + ra2_in[d - 1]
-    for d in (1, 3, 2):
-        rb2_copy(d).wait_recv()
+    fb_src[z, 0:72, :] = first
+    for d in (1, 3, 2):
+        start(fz_copy(z, 0, d))
+    last = rb_sum[x]
+    take_group(rb2_in, rs_s.at[3], rs_r.at[3])
+    for d in (1, 3, 2):
         last = last + rb2_in[d - 1]
-    fb_src[z, 0:72, :] = first
     fb_src[z, 72:144, :] = last
-
-    def fz_copy(d):
-        return copy(fb_src.at[z], fb_src.at[z], fz_s.at[d - 1], fz_r.at[d - 1], znext(d))
+    for d in (1, 3, 2):
+        start(fz_copy(z, 1, d))
 
     def fb_copy(c, h):
         return copy(fb_src.at[c], fb_buf.at[j * 2 + yh], fb_s.at[c, h], fb_r.at[j * 2 + yh],
@@ -659,12 +664,11 @@
                     fb_copy(c, h).wait_send()
 
     sent.append(fb_gone)
-    for d in (1, 3, 2):
-        start(fz_copy(d))
     fb_send(z)
     for d in (1, 3, 2):
         c = lax.rem(z + 4 - d, 4)
-        copy(fb_src.at[c], fb_src.at[c], fz_s.at[d - 1], fz_r.at[d - 1], partner).wait_recv()
+        fz_copy(c, 0, d).wait_recv()
+        fz_copy(c, 1, d).wait_recv()
         fb_send(c)
     fb_buf[j * 2 + yh] = fb_src[j]
 
@@ -684,8 +688,9 @@
             lanes = slice(g * 128, (g + 1) * 128)
             grads_out[0, rows, lanes] = acc[rows, lanes] - tt_all[h * 4 + g]
 
+    take_group(loss_a, la_s.at[0], la_r.at[0])
+
     def la_wait(d, acc):
-        la_copy(d).wait_recv()
         return acc + loss_a[d - 1]
 
     whole = lax.fori_loop(1, 8, la_wait, loss_src2[...])
@@ -749,12 +754,11 @@
             dma((4,)), dma((2, 3, 2)), dma((2, 3, 2)),
             dma((2, 3)), dma((2,)), dma((2, 3)), dma((2, 3)), dma((2, 4)), dma((2, 4)),
             dma((2, 2)), dma((2, 2)), dma((3,)), dma((3,)),
-            dma((1,)), dma((1,)), dma((3,)), dma((3,)), dma((3,)), dma((3,)), dma((7,)), dma((8,)),
-            dma((15,)), dma((15,)),
-            dma((2, 3)), dma((2, 3)), dma((2, 3)), dma((2, 3)), dma((2, 3)), dma((2, 3)),
+            dma((1,)), dma((1,)), dma((3,)), dma((3,)), dma((1,)), dma((1,)), dma((7,)), dma((8,)),
+            dma((1,)), dma((1,)), dma((2,)), dma((2,)), dma((2,)), dma((2,)), dma((2,)), dma((2,)),
             dma((3,)), dma((3,)), dma((3, 2)), dma((3, 2)), dma((2,)), dma((2,)),
-            dma((4, 3)), dma((4, 3)), dma((3,)), dma((3,)), dma((4, 2)), dma((8,)),
-            dma((15,)), dma((15,)), dma((7,)), dma((7,)),
+            dma((4,)), dma((4,)), dma((2, 3)), dma((2, 3)), dma((4, 2)), dma((8,)),
+            dma((1,)), dma((1,)), dma((1,)), dma((1,)),
         ],
         compiler_params=pltpu.CompilerParams(
             collective_id=0, has_side_effects=True, vmem_limit_bytes=58 * 1024 * 1024

time: 103 us -> 102 us (level); the launches traced: 102 us -> 100 us
  Pallas kernels: 98.9 us -> 96.7 us
    pallas_call x1, Pallas kernels: 98.9 us -> 96.7 us  [per_device(): pl.pallas_call(kernel, name='distill', out_shape=(jax.ShapeDtypeStruct((1...]
where the time goes in v7:
time: 102 us; the launch traced here: 100 us
  Pallas kernels  96.7 us (95%)
  between operations  2.4 us (2%)
  other arithmetic  1.14 us (1%)
    pallas_call x1, Pallas kernels, per_device(): pl.pallas_call(kernel, name='distill', out_shape=(jax.ShapeDtypeStruct((1...  96.7 us

profile of v7, /device:TPU:97, one launch (start us, length us, event | category | flops | bytes accessed | tf_op | source)
XLA Modules:
  0.0 100.2 jit_solution(1353190849869876242)
XLA Ops:
  0.6 96.7 %distill.1 = (f32[1,1]{1,0:T(1,128)}, f32[2,288,512]{2,1,0:T(8,128)S(1)}) custom-call(bf16[288,512]{1,0:T(8,128)(2,1)} %bitcast.6, bf16[288,512]{1,0:T(8,128)(2,1)} %stext.1, bf16[288,1280]{1,0:T(8,128)(2,1)} %bitcast.5, bf16[288,1280]{1,0:T(8,128)(2,1)} %ttext.1), custom_call_target="tpu_custom_call" | custom-call | flops 8000000000 | bytes 4194304 | tf_op jit(solution)/shard_map/distill/pallas_call | solution.py:721
  97.3 1.1 %multiply_bitcast_fusion = (f32[288,512]{1,0:T(8,128)}, f32[1,288,512]{2,1,0:T(8,128)}) fusion(f32[2,288,512]{2,1,0:T(8,128)S(1)} %get-tuple-element.6), kind=kLoop, calls=%fused_computation | loop fusion | flops 294912 | bytes 2359296 | tf_op jit(solution)/shard_map/mul | solution.py:771

commit v8 on v7

--- a/solution.py
+++ b/solution.py
@@ -80,6 +80,9 @@
             c.start()
         sent.append(copy(into, into, ss, rs, sib).wait_send)
 
+    def sent_in_all(ref, ss, rs):
+        sent.append(copy(ref, ref, ss, rs, sib).wait_send)
+
     def take_group(into, ss, rs):
         copy(into, into, ss, rs, sib).wait_recv()
 
@@ -112,37 +115,38 @@
 
     def img_send(m, d, h):
         return copy(
-            own[m].at[half(h)], imgs[m].at[z, half(h)], zi_s.at[m, d, h], zi_r.at[m, d, h],
+            own[m].at[half(h)], imgs[m].at[z, half(h)], zi_s.at[m], zi_r.at[m, d, h],
             znext(1 if d == 0 else 3),
         )
 
     def img_relay(m, d):
         slot = zm1 if d == 0 else zp1
         ref = imgs[m].at[slot, half(d)]
-        return copy(ref, ref, zi_s.at[m, 2, d], zi_r.at[m, 2, d], znext(1 if d == 0 else 3))
+        return copy(ref, ref, zi_s.at[m], zi_r.at[m, 2, d], znext(1 if d == 0 else 3))
 
     def img_recv(m, d, h):
         slot = zm1 if d == 0 else zp1
         ref = imgs[m].at[slot, half(h)]
-        copy(ref, ref, zi_s.at[m, d, h], zi_r.at[m, d, h], znext(1)).wait_recv()
+        copy(ref, ref, zi_s.at[m], zi_r.at[m, d, h], znext(1)).wait_recv()
 
     def img_recv_far(m, d):
         ref = imgs[m].at[zp2, half(d)]
-        copy(ref, ref, zi_s.at[m, 2, d], zi_r.at[m, 2, d], znext(1)).wait_recv()
+        copy(ref, ref, zi_s.at[m], zi_r.at[m, 2, d], znext(1)).wait_recv()
 
     def img_start(m):
-        start(img_send(m, 0, 0))
-        start(img_send(m, 1, 1))
+        img_send(m, 0, 0).start()
+        img_send(m, 1, 1).start()
 
     def img_rest(m):
-        start(img_send(m, 0, 1))
-        start(img_send(m, 1, 0))
+        img_send(m, 0, 1).start()
+        img_send(m, 1, 0).start()
 
     def img_pass_on(m):
         img_recv(m, 0, 0)
-        start(img_relay(m, 0))
+        img_relay(m, 0).start()
         img_recv(m, 1, 1)
-        start(img_relay(m, 1))
+        img_relay(m, 1).start()
+        sent_in_all(imgs[m].at[0:3], zi_s.at[m], zi_r.at[m, 2, 1])
 
     syl, sk = z // 2, z % 2
     is_source = j == z
@@ -445,18 +449,18 @@
         gsend[d] = dot(w[v], ts[...], NN)
 
     def g_far(h):
-        return copy(gsend.at[2, half(h)], gfar_in.at[h], g_s.at[2, h], g_r.at[2, h],
+        return copy(gsend.at[2, half(h)], gfar_in.at[h], g_s.at[0], g_r.at[2, h],
                     znext(1 if h == 0 else 3))
 
     def g_copy(i, h):
         d = 1 + 2 * i
-        return copy(gsend.at[d, half(h)], grecv.at[i, half(h)], g_s.at[i, h], g_r.at[i, h],
+        return copy(gsend.at[d, half(h)], grecv.at[i, half(h)], g_s.at[0], g_r.at[i, h],
                     znext(d))
 
-    start(g_far(0))
-    start(g_far(1))
-    start(g_copy(0, 1))
-    start(g_copy(1, 0))
+    g_far(0).start()
+    g_far(1).start()
+    g_copy(0, 1).start()
+    g_copy(1, 0).start()
 
 
     stats_finish(0)
@@ -496,7 +500,8 @@
         g_far(i).wait_recv()
         rows = slice(i * HALF, (i + 1) * HALF)
         gsend[1 + 2 * i, rows] = gsend[1 + 2 * i, rows] + gfar_in[i]
-        start(g_copy(i, i))
+        g_copy(i, i).start()
+    sent_in_all(gsend.at[1:4], g_s.at[0], g_r.at[0, 0])
 
     for n in range(NCH):
         tgt_copy(n).wait_recv()
@@ -582,20 +587,20 @@
 
     a_in = (1 - yh) * 4 + z
     ty = copy(tt_src, tt_all.at[a], ta_s.at[0], ta_r.at[a], partner)
-    start(ty)
+    ty.start()
     rb_copy(2).start()
 
     def ta_copy(d):
-        return copy(tt_src, tt_all.at[a], ta_s.at[d], ta_r.at[a], znext(d))
+        return copy(tt_src, tt_all.at[a], ta_s.at[0], ta_r.at[a], znext(d))
 
     def tb_copy(d):
-        return copy(tt_all.at[a_in], tt_all.at[a_in], ta_s.at[3 + d], ta_r.at[a_in], znext(d))
+        return copy(tt_all.at[a_in], tt_all.at[a_in], ta_s.at[0], ta_r.at[a_in], znext(d))
 
     def t_wait(slot):
         copy(tt_src, tt_all.at[slot], ta_s.at[0], ta_r.at[slot], partner).wait_recv()
 
     for d in (1, 3, 2):
-        start(ta_copy(d))
+        ta_copy(d).start()
     tt_all[a] = total
 
     take_group(loss_b, lb_s.at[0], lb_r.at[0])
@@ -623,10 +628,11 @@
     start_group([rb2_copy(d) for d in (1, 3, 2)], rb2_in, rs_s.at[3], rs_r.at[3])
     t_wait(a_in)
     for d in (1, 3, 2):
-        start(tb_copy(d))
+        tb_copy(d).start()
+    sent_in_all(tt_all.at[0:7], ta_s.at[0], ta_r.at[0])
     def fz_copy(c, i, d):
         ref = fb_src.at[c, i * 72 : (i + 1) * 72]
-        return copy(ref, ref, fz_s.at[i, d - 1], fz_r.at[i, d - 1], znext(d))
+        return copy(ref, ref, fz_s.at[0], fz_r.at[i, d - 1], znext(d))
 
     first = ra_sum[y]
     take_group(ra2_in, rs_s.at[2], rs_r.at[2])
@@ -634,14 +640,15 @@
         first = first + ra2_in[d - 1]
     fb_src[z, 0:72, :] = first
     for d in (1, 3, 2):
-        start(fz_copy(z, 0, d))
+        fz_copy(z, 0, d).start()
     last = rb_sum[x]
     take_group(rb2_in, rs_s.at[3], rs_r.at[3])
     for d in (1, 3, 2):
         last = last + rb2_in[d - 1]
     fb_src[z, 72:144, :] = last
     for d in (1, 3, 2):
-        start(fz_copy(z, 1, d))
+        fz_copy(z, 1, d).start()
+    sent_in_all(fb_src.at[0:3], fz_s.at[0], fz_r.at[0, 0])
 
     def fb_copy(c, h):
         return copy(fb_src.at[c], fb_buf.at[j * 2 + yh], fb_s.at[c, h], fb_r.at[j * 2 + yh],
@@ -751,13 +758,13 @@
             V((2, 3, 8, COLS), F32), V((2, 8, COLS), F32),
             V((2, COLS), F32), V((15, 2, COLS), F32),
             V((8, 128), F32), V((15, 8, 128), F32), V((8, 128), F32), V((7, 8, 128), F32),
-            dma((4,)), dma((2, 3, 2)), dma((2, 3, 2)),
+            dma((4,)), dma((2,)), dma((2, 3, 2)),
             dma((2, 3)), dma((2,)), dma((2, 3)), dma((2, 3)), dma((2, 4)), dma((2, 4)),
             dma((2, 2)), dma((2, 2)), dma((3,)), dma((3,)),
-            dma((1,)), dma((1,)), dma((3,)), dma((3,)), dma((1,)), dma((1,)), dma((7,)), dma((8,)),
+            dma((1,)), dma((1,)), dma((3,)), dma((3,)), dma((1,)), dma((1,)), dma((1,)), dma((8,)),
             dma((1,)), dma((1,)), dma((2,)), dma((2,)), dma((2,)), dma((2,)), dma((2,)), dma((2,)),
-            dma((3,)), dma((3,)), dma((3, 2)), dma((3, 2)), dma((2,)), dma((2,)),
-            dma((4,)), dma((4,)), dma((2, 3)), dma((2, 3)), dma((4, 2)), dma((8,)),
+            dma((3,)), dma((3,)), dma((1,)), dma((3, 2)), dma((2,)), dma((2,)),
+            dma((4,)), dma((4,)), dma((1,)), dma((2, 3)), dma((4, 2)), dma((8,)),
             dma((1,)), dma((1,)), dma((1,)), dma((1,)),
         ],
         compiler_params=pltpu.CompilerParams(

time: 102 us -> 102 us (level)
  no operation moved by 1% of the time
where the time goes in v8:
time: 102 us; the launch traced here: 99.9 us
  Pallas kernels  96.4 us (95%)
  between operations  2.4 us (2%)
  other arithmetic  1.14 us (1%)
    pallas_call x1, Pallas kernels, per_device(): pl.pallas_call(kernel, name='distill', out_shape=(jax.ShapeDtypeStruct((1...  96.4 us

profile of v8, /device:TPU:97, one launch (start us, length us, event | category | flops | bytes accessed | tf_op | source)
XLA Modules:
  0.0 99.9 jit_solution(5032861805582500523)
XLA Ops:
  0.6 96.4 %distill.1 = (f32[1,1]{1,0:T(1,128)}, f32[2,288,512]{2,1,0:T(8,128)S(1)}) custom-call(bf16[288,512]{1,0:T(8,128)(2,1)} %bitcast.6, bf16[288,512]{1,0:T(8,128)(2,1)} %stext.1, bf16[288,1280]{1,0:T(8,128)(2,1)} %bitcast.5, bf16[288,1280]{1,0:T(8,128)(2,1)} %ttext.1), custom_call_target="tpu_custom_call" | custom-call | flops 8000000000 | bytes 4194304 | tf_op jit(solution)/shard_map/distill/pallas_call | solution.py:728
  97.0 1.1 %multiply_bitcast_fusion = (f32[288,512]{1,0:T(8,128)}, f32[1,288,512]{2,1,0:T(8,128)}) fusion(f32[2,288,512]{2,1,0:T(8,128)S(1)} %get-tuple-element.6), kind=kLoop, calls=%fused_computation | loop fusion | flops 294912 | bytes 2359296 | tf_op jit(solution)/shard_map/mul | solution.py:778

commit v9 on v8

--- a/solution.py
+++ b/solution.py
@@ -205,7 +205,7 @@
 
     def text_sib(m, d):
         blk = lax.rem(x + 4 - d, 4)
-        return copy(tslab(m, blk, k), tslab(m, blk, k), t3_s.at[m, d], t3_r.at[m, d], sib)
+        return copy(tslab(m, blk, k), tslab(m, blk, k), t3_s.at[m], t3_r.at[m, d], sib)
 
     holds = yl == syl
     lacks = yl != syl
@@ -233,7 +233,9 @@
         for d in (1, 3):
             if m == 0 or here is holds:
                 start_if(here, text_x(m, d))
-        start_if(here, text_sib(m, 0))
+        @pl.when(here)
+        def _():
+            text_sib(m, 0).start()
 
     def text_pass_on(m):
         for d in (1, 3):
@@ -248,7 +250,7 @@
             else:
                 text_got(m, d)
                 start(text_relay(m, d // 2))
-            start(text_sib(m, d))
+            text_sib(m, d).start()
 
     def text_far(m):
         def arrived():
@@ -262,12 +264,13 @@
             crossed(2)
         else:
             arrived()
-        start(text_sib(m, 2))
+        text_sib(m, 2).start()
+        sent_in_all(texts[m].at[0 : 2 * ROWS], t3_s.at[m], t3_r.at[m, 0])
 
     def text_wait(m):
         for d in range(4):
             blk = lax.rem(x + 4 - d, 4)
-            copy(tslab(m, blk, 1 - k), tslab(m, blk, 1 - k), t3_s.at[m, d], t3_r.at[m, d],
+            copy(tslab(m, blk, 1 - k), tslab(m, blk, 1 - k), t3_s.at[m], t3_r.at[m, d],
                  sib).wait_recv()
 
     lane = lax.broadcasted_iota(jnp.int32, (ROWS, 128), 1)
@@ -418,8 +421,8 @@
     img_recv_far(0, 0)
     img_recv_far(0, 1)
     scores(0, zp2, pt, qt, teacher_scale, far=True)
+    rows_start(0)
     start_all(1, 16, far_copy, cfar_in, far_s.at[0], far_r.at[0])
-    rows_start(0)
 
     def iz_copy(d):
         slot = isum_in.at[z]
@@ -651,7 +654,7 @@
     sent_in_all(fb_src.at[0:3], fz_s.at[0], fz_r.at[0, 0])
 
     def fb_copy(c, h):
-        return copy(fb_src.at[c], fb_buf.at[j * 2 + yh], fb_s.at[c, h], fb_r.at[j * 2 + yh],
+        return copy(fb_src.at[c], fb_buf.at[j * 2 + yh], fb_s.at[0], fb_r.at[j * 2 + yh],
                     dev(x, c, h, z))
 
     def is_self(c, h):
@@ -663,14 +666,7 @@
             def _():
                 fb_copy(c, h).start()
 
-    def fb_gone():
-        for c in range(4):
-            for h in range(2):
-                @pl.when(jnp.logical_not(is_self(c, h)))
-                def _():
-                    fb_copy(c, h).wait_send()
-
-    sent.append(fb_gone)
+    sent_in_all(fb_buf.at[0:7], fb_s.at[0], fb_r.at[0])
     fb_send(z)
     for d in (1, 3, 2):
         c = lax.rem(z + 4 - d, 4)
@@ -706,7 +702,7 @@
     def fb_wait(s, _):
         @pl.when(s != j * 2 + yh)
         def _():
-            copy(fb_src.at[0], fb_buf.at[s], fb_s.at[0, 0], fb_r.at[s], partner).wait_recv()
+            copy(fb_src.at[0], fb_buf.at[s], fb_s.at[0], fb_r.at[s], partner).wait_recv()
 
         return 0
 
@@ -759,12 +755,12 @@
             V((2, COLS), F32), V((15, 2, COLS), F32),
             V((8, 128), F32), V((15, 8, 128), F32), V((8, 128), F32), V((7, 8, 128), F32),
             dma((4,)), dma((2,)), dma((2, 3, 2)),
-            dma((2, 3)), dma((2,)), dma((2, 3)), dma((2, 3)), dma((2, 4)), dma((2, 4)),
+            dma((2, 3)), dma((2,)), dma((2, 3)), dma((2, 3)), dma((2,)), dma((2, 4)),
             dma((2, 2)), dma((2, 2)), dma((3,)), dma((3,)),
             dma((1,)), dma((1,)), dma((3,)), dma((3,)), dma((1,)), dma((1,)), dma((1,)), dma((8,)),
             dma((1,)), dma((1,)), dma((2,)), dma((2,)), dma((2,)), dma((2,)), dma((2,)), dma((2,)),
             dma((3,)), dma((3,)), dma((1,)), dma((3, 2)), dma((2,)), dma((2,)),
-            dma((4,)), dma((4,)), dma((1,)), dma((2, 3)), dma((4, 2)), dma((8,)),
+            dma((4,)), dma((4,)), dma((1,)), dma((2, 3)), dma((1,)), dma((8,)),
             dma((1,)), dma((1,)), dma((1,)), dma((1,)),
         ],
         compiler_params=pltpu.CompilerParams(

time: 102 us -> 102 us (level)
  no operation moved by 1% of the time
where the time goes in v9:
time: 102 us; the launch traced here: 100 us
  Pallas kernels  96.6 us (95%)
  between operations  2.4 us (2%)
  other arithmetic  1.14 us (1%)
    pallas_call x1, Pallas kernels, per_device(): pl.pallas_call(kernel, name='distill', out_shape=(jax.ShapeDtypeStruct((1...  96.6 us

profile of v9, /device:TPU:97, one launch (start us, length us, event | category | flops | bytes accessed | tf_op | source)
XLA Modules:
  0.0 100.2 jit_solution(4371120889070368504)
XLA Ops:
  0.6 96.6 %distill.1 = (f32[1,1]{1,0:T(1,128)}, f32[2,288,512]{2,1,0:T(8,128)S(1)}) custom-call(bf16[288,512]{1,0:T(8,128)(2,1)} %bitcast.6, bf16[288,512]{1,0:T(8,128)(2,1)} %stext.1, bf16[288,1280]{1,0:T(8,128)(2,1)} %bitcast.5, bf16[288,1280]{1,0:T(8,128)(2,1)} %ttext.1), custom_call_target="tpu_custom_call" | custom-call | flops 8000000000 | bytes 4194304 | tf_op jit(solution)/shard_map/distill/pallas_call | solution.py:724
  97.3 1.1 %multiply_bitcast_fusion = (f32[288,512]{1,0:T(8,128)}, f32[1,288,512]{2,1,0:T(8,128)}) fusion(f32[2,288,512]{2,1,0:T(8,128)S(1)} %get-tuple-element.6), kind=kLoop, calls=%fused_computation | loop fusion | flops 294912 | bytes 2359296 | tf_op jit(solution)/shard_map/mul | solution.py:774
